TPU v7x, 256 devices: a whole 4x4x8 slice. The times are simulated.
256 devices in a mesh: slab: 32 (over y, x, core), grp: 8 (over z).
Axes of the slice: x: 4, y: 4, z: 8, core: 2. Of those that a mesh axis runs over, the one named last changes fastest.
Arguments:
- right_side: float32 [64, 32768], P(None, ('slab', 'grp')), may hold values from -45 to 45
- stiffness: bfloat16 [7, 64, 64, 32768], P(None, None, None, ('slab', 'grp')), may hold values from -1 to 3.5
- columns: int32 [7, 32768], P(None, ('slab', 'grp')), may hold values from 0 to 1087, as said below
- margin_rows: int32 [32, 2, 32], P('slab'), may hold values from 0 to 1023, as said below
- local_inverse: bfloat16 [64, 64, 32768], P(None, None, ('slab', 'grp')), may hold values from -1 to 1.5
- margin_inverse: bfloat16 [64, 64, 2048], P(None, None, 'slab'), may hold values from -1 to 1.5
- basis: bfloat16 [64, 64, 32768], P(None, None, ('slab', 'grp')), may hold values from -0.0234375 to 0.0234375
- coarse_counts: int32 [32], P('slab'), may hold values from 32 to 64
- coarse_inverse: float32 [2048, 2048], P('slab'), may hold values from -65 to 65
Outputs:
- solution_field: float32 [64, 32768], P(None, ('slab', 'grp'))
- residual: float32 [64, 32768], P(None, ('slab', 'grp'))
- direction: float32 [64, 32768], P(None, ('slab', 'grp'))
Inputs may be any that keep to these rules, and one draw needn't show every extreme that they name: Entry 0 of block row b names the row itself; every position of the last 32 columns of ext_s is named by some row of slab s, and so is every position of the first 32. margin_rows[s, 0] holds 32 distinct rows of the lowest quarter of slab s, margin_rows[s, 1] 32 distinct rows of its highest quarter.
All inputs are finite; a program needn't handle non-finite values.
Results may differ from a plain program's by a relative error of at most 0.0003.
Values sent between devices are 32-bit elements; how exact they have to be, the bound alone decides.
No kernel may reach another device: no remote copies, remote signals or barrier semaphores. Data moves between devices by JAX's collectives and lax.ppermute only.
A program may use at most 64 MiB of HBM per device.

v0:
```python
import jax
import jax.numpy as jnp
from jax import lax
from jax.sharding import PartitionSpec as P

ITERS = 2


precise = lax.Precision.HIGHEST


def padded_2(value, sides, width):
    for axis, dim in sides:
        peers, length = (lax.axis_size(axis), value.shape[dim])
        up = [(i, (i + 1) % peers) for i in range(peers - 1)]
        down = [(j, i) for i, j in up]
        last = lax.slice_in_dim(value, length - width, length, axis=dim)
        initial = lax.slice_in_dim(value, 0, width, axis=dim)
        before = lax.ppermute(last, axis, up)
        after = lax.ppermute(initial, axis, down)
        value = jnp.concatenate([before, value, after], axis=dim)
    return value


def local(
    right_side,
    stiffness,
    columns,
    margin_rows,
    local_inverse,
    margin_inverse,
    basis,
    coarse_counts,
    coarse_inverse,
):
    face_width = margin_rows.shape[2]
    rows_dev = right_side.shape[1]
    coarse_width = basis.shape[0]
    sent_lists = jnp.concatenate([margin_rows[0, 0], margin_rows[0, 1]])
    offsets = sent_lists - lax.axis_index("grp") * rows_dev
    select = (offsets[:, None] == jnp.arange(rows_dev, dtype=jnp.int32)[None, :]).astype(
        jnp.float32
    )
    live_slots = (jnp.arange(coarse_width, dtype=jnp.int32) < coarse_counts[0]).astype(jnp.float32)

    def gather_slab(vector):
        return lax.all_gather(vector, "grp", axis=1, tiled=True)

    def exchange_faces(outgoing):
        return padded_2(outgoing, (("slab", 1),), face_width)

    def split_rims(padded):
        return (padded[:, :face_width], padded[:, 3 * face_width :])

    def precondition(vector):
        outgoing = jnp.take(gather_slab(vector), sent_lists, axis=1)
        lower_rim, upper_rim = split_rims(exchange_faces(outgoing))
        local_part = jnp.einsum(
            "ijb,jb->ib",
            local_inverse,
            vector,
            precision=precise,
            preferred_element_type=jnp.float32,
        )
        facing = jnp.concatenate([lower_rim, upper_rim], axis=1)
        solved = jnp.einsum(
            "ijb,jb->ib",
            margin_inverse,
            facing,
            precision=precise,
            preferred_element_type=jnp.float32,
        )
        returning = padded_2(solved, (("slab", 1),), face_width)
        from_below, from_above = split_rims(returning)
        returned = jnp.dot(
            jnp.concatenate([from_below, from_above], axis=1), select, precision=precise
        )
        projected = (
            jnp.einsum(
                "jib,ib->j", basis, vector, precision=precise, preferred_element_type=jnp.float32
            )
            * live_slots
        )
        pieces = lax.all_gather(projected, ("slab", "grp"), axis=0, tiled=True)
        gathered = (
            pieces.reshape(lax.axis_size("slab"), lax.axis_size("grp"), coarse_width)
            .sum(axis=1)
            .reshape(-1)
        )
        weights = jnp.dot(coarse_inverse, gathered, precision=precise) * live_slots
        coarse_part = jnp.einsum(
            "jib,j->ib", basis, weights, precision=precise, preferred_element_type=jnp.float32
        )
        return local_part + returned + coarse_part

    def single_total(first_vec, second_vec):
        return lax.psum(jnp.sum(first_vec * second_vec), ("slab", "grp"))

    solution_field = jnp.zeros_like(right_side)
    residual = right_side
    search = precondition(residual)
    direction = search
    energy = single_total(residual, search)
    for iteration in range(ITERS):
        slab_values = gather_slab(direction)
        apply_lower_rim, apply_upper_rim = split_rims(
            exchange_faces(jnp.take(slab_values, sent_lists, axis=1))
        )
        extended = jnp.concatenate([apply_lower_rim, slab_values, apply_upper_rim], axis=1)
        picked = jnp.take(extended, columns, axis=1)
        image = jnp.einsum(
            "kijb,jkb->ib", stiffness, picked, precision=precise, preferred_element_type=jnp.float32
        )
        step_size = energy / single_total(direction, image)
        solution_field = solution_field + step_size * direction
        residual = residual - step_size * image
        search = precondition(residual)
        energy_next = single_total(residual, search)
        direction = search + energy_next / energy * direction
        energy = energy_next
    return (solution_field, residual, direction)


def solution(mesh):
    in_specs = (
        P(None, ("slab", "grp")),
        P(None, None, None, ("slab", "grp")),
        P(None, ("slab", "grp")),
        P("slab", None, None),
        P(None, None, ("slab", "grp")),
        P(None, None, "slab"),
        P(None, None, ("slab", "grp")),
        P("slab"),
        P("slab", None),
    )
    out_specs = (P(None, ("slab", "grp")), P(None, ("slab", "grp")), P(None, ("slab", "grp")))
    return jax.shard_map(local, mesh=mesh, in_specs=in_specs, out_specs=out_specs, check_vma=False)
```

profile of v0, /device:TPU:1, one launch (start us, length us, event | category | flops | bytes accessed | tf_op | source)
XLA Modules:
  0.0 1236.6 jit_solution(10924661813084758457)
XLA Ops:
  9.0 23.7 %all_gather.24 = f32[64,1024]{0,1:T(8,128)S(1)} all-gather(f32[64,128]{0,1:T(8,128)S(1)} %copy.21), channel_id=1, replica_groups=mesh['slab'=32,'grp'=8] {'grp'}, dimensions={1}, use_global_device_ids=true | all-gather | bytes 294912 | tf_op jit(solution)/shard_map/all_gather | solution.py:47
  33.4 9.9 collective-permute-start
  43.3 1.9 collective-permute-start.1
  45.9 2.5 fusion.8
  50.8 1.6 fusion.2
  52.4 3.3 copy.37
  55.8 0.9 fusion.54
  56.7 3.6 collective-permute-start.2
  60.4 1.9 collective-permute-start.3
  62.3 224.4 %all-reduce.8.cloned.1.call-done = f32[16384]{0:T(1024)} async-done(((f32[16384]{0:T(1024)}), f32[16384]{0:T(1024)}) %all-reduce.8.cloned.1.call-update) | async-done | bytes 65552
  286.7 0.9 reshape.51
  288.3 1.0 fusion.23
  289.6 18.8 %all_gather.26 = f32[64,1024]{1,0:T(8,128)S(1)} all-gather(f32[64,128]{1,0:T(8,128)S(1)} %fusion.7), channel_id=1, replica_groups=mesh['slab'=32,'grp'=8] {'grp'}, dimensions={1}, use_global_device_ids=true | all-gather | bytes 294912 | tf_op jit(solution)/shard_map/all_gather | solution.py:47
  309.3 8.5 collective-permute-start.4
  317.9 1.9 collective-permute-start.5
  319.8 3.3 collective-permute-done.5
  323.5 2.8 gather_fusion.2
  326.3 1.2 select_bitcast_fusion.1
  327.7 5.0 fusion
  333.3 76.5 %all-reduce.3 = (f32[]{:T(128)}, f32[]{:T(128)}) all-reduce(f32[]{:T(128)} %get-tuple-element.6, f32[]{:T(128)} %get-tuple-element.5), channel_id=1, replica_groups=mesh['slab'=32,'grp'=8] {'slab','grp'}, use_global_device_ids=true, to_apply=%region_2.4 | all-reduce | flops 2 | bytes 16 | tf_op jit(solution)/shard_map/psum | solution.py:97
  411.2 18.8 %all_gather.27 = f32[64,1024]{1,0:T(8,128)S(1)} all-gather(f32[64,128]{1,0:T(8,128)S(1)} %fusion.38), channel_id=1, replica_groups=mesh['slab'=32,'grp'=8] {'grp'}, dimensions={1}, use_global_device_ids=true | all-gather | bytes 294912 | tf_op jit(solution)/shard_map/all_gather | solution.py:47
  430.9 9.4 collective-permute-start.6
  440.3 2.1 collective-permute-start.7
  442.4 1.3 fusion.9
  445.4 2.1 fusion.55
  447.5 3.3 collective-permute-start.8
  450.8 1.9 collective-permute-start.9
  452.8 227.5 %all-reduce.10.cloned.1.call-done = f32[16384]{0:T(1024)} async-done(((f32[16384]{0:T(1024)}), f32[16384]{0:T(1024)}) %all-reduce.10.cloned.1.call-update) | async-done | bytes 65552
  681.9 1.0 fusion.20
  683.7 74.3 %psum.37 = f32[]{:T(128)} all-reduce(f32[]{:T(128)} %get-tuple-element.31), channel_id=1, replica_groups=mesh['slab'=32,'grp'=8] {'slab','grp'}, use_global_device_ids=true, to_apply=%region_7.10 | all-reduce | flops 1 | bytes 8 | tf_op jit(solution)/shard_map/psum | solution.py:97
  760.0 18.9 %all_gather.29 = f32[64,1024]{1,0:T(8,128)S(1)} all-gather(f32[64,128]{1,0:T(8,128)S(1)} %multiply_add_fusion.2), channel_id=1, replica_groups=mesh['slab'=32,'grp'=8] {'grp'}, dimensions={1}, use_global_device_ids=true | all-gather | bytes 294912 | tf_op jit(solution)/shard_map/all_gather | solution.py:47
  779.8 8.2 collective-permute-start.10
  788.1 1.9 collective-permute-start.11
  790.0 3.3 collective-permute-done.11
  793.7 2.8 gather_fusion.5
  796.5 1.2 select_bitcast_fusion
  797.9 5.0 fusion.1
  803.5 77.2 %psum.38 = f32[]{:T(128)} all-reduce(f32[]{:T(128)} %fusion.35), channel_id=1, replica_groups=mesh['slab'=32,'grp'=8] {'slab','grp'}, use_global_device_ids=true, to_apply=%region_9.12 | all-reduce | flops 1 | bytes 8 | tf_op jit(solution)/shard_map/psum | solution.py:97
  882.1 18.8 %all_gather.30 = f32[64,1024]{1,0:T(8,128)S(1)} all-gather(f32[64,128]{1,0:T(8,128)S(1)} %fusion.36), channel_id=1, replica_groups=mesh['slab'=32,'grp'=8] {'grp'}, dimensions={1}, use_global_device_ids=true | all-gather | bytes 294912 | tf_op jit(solution)/shard_map/all_gather | solution.py:47
  901.8 8.5 collective-permute-start.12
  910.3 2.1 collective-permute-start.13
  912.5 1.3 fusion.10
  915.4 2.1 fusion.56
  917.5 3.3 collective-permute-start.14
  920.9 1.9 collective-permute-start.15
  922.8 227.5 %all-reduce.12.cloned.1.call-done = f32[16384]{0:T(1024)} async-done(((f32[16384]{0:T(1024)}), f32[16384]{0:T(1024)}) %all-reduce.12.cloned.1.call-update) | async-done | bytes 65552
  1151.9 1.0 fusion.17
  1153.7 74.3 %psum.39 = f32[]{:T(128)} all-reduce(f32[]{:T(128)} %get-tuple-element.33), channel_id=1, replica_groups=mesh['slab'=32,'grp'=8] {'slab','grp'}, use_global_device_ids=true, to_apply=%region_12.15 | all-reduce | flops 1 | bytes 8 | tf_op jit(solution)/shard_map/psum | solution.py:97
  (117 shorter events, 21.2 us)
Async XLA Ops:
  7.2 280.6 %copy-start = (f32[64,2048]{1,0:T(8,128)S(1)}, f32[64,2048]{1,0:T(8,128)}, u32[]{:S(2)}) copy-start(f32[64,2048]{1,0:T(8,128)} %param.21) | copy-start | bytes 1572868
  7.2 281.1 %copy-start.2 = (bf16[64,64,128]{2,1,0:T(8,128)(2,1)S(1)}, bf16[64,64,128]{2,1,0:T(8,128)(2,1)}, u32[]{:S(2)}) copy-start(bf16[64,64,128]{2,1,0:T(8,128)(2,1)} %param.19) | copy-start | bytes 3145732
  7.2 279.5 %all-reduce.8.cloned.1.call-start = ((), (), s32[]{:S(2)}) async-start(), calls=%async_computation | async-start | bytes 131072
  33.4 22.3 %collective-permute-start = (f32[64,32]{0,1:T(8,128)S(1)}, f32[64,32]{0,1:T(8,128)S(1)}, u32[]{:S(2)}, u32[]{:S(2)}) collective-permute-start(f32[64,32]{0,1:T(8,128)S(1)} %get-tuple-element.27), channel_id=1, source_target_pairs={{0,8},{8,16},{16,24},{24,32},{32,40},{40,48},{48,56},{56,64},{64,7... | collective-permute-start | bytes 24584 | tf_op jit(solution)/shard_map/ppermute | solution.py:19
  43.3 12.5 %collective-permute-start.1 = (f32[64,32]{0,1:T(8,128)S(1)}, f32[64,32]{0,1:T(8,128)S(1)}, u32[]{:S(2)}, u32[]{:S(2)}) collective-permute-start(f32[64,32]{0,1:T(8,128)S(1)} %get-tuple-element.28), channel_id=1, source_target_pairs={{8,0},{16,8},{24,16},{32,24},{40,32},{48,40},{56,48},{64,56},{72,6... | collective-permute-start | bytes 24584 | tf_op jit(solution)/shard_map/ppermute | solution.py:20
  48.7 0.6 copy-start.9
  49.3 631.0 %all-reduce.10.cloned.1.call-start = ((), (), s32[]{:S(2)}) async-start(), calls=%async_computation.1 | async-start | bytes 131072
  52.4 265.4 %copy-start.11 = (s32[64]{0:T(128)}, s32[64]{0:T(128)S(1)}, u32[]{:S(2)}) copy-start(s32[64]{0:T(128)S(1)} %broadcast_subtract_fusion) | copy-start | bytes 772
  55.7 233.5 %copy-start.3 = (bf16[64,64,64]{0,1,2:T(8,128)(2,1)}, bf16[64,64,64]{0,1,2:T(8,128)(2,1)S(1)}, u32[]{:S(2)}) copy-start(bf16[64,64,64]{0,1,2:T(8,128)(2,1)S(1)} %copy.37) | copy-start | bytes 1572868
  56.7 232.5 %collective-permute-start.2 = (f32[64,32]{0,1:T(8,128)S(1)}, f32[64,32]{0,1:T(8,128)S(1)}, u32[]{:S(2)}, u32[]{:S(2)}) collective-permute-start(f32[64,32]{0,1:T(8,128)S(1)} %get-tuple-element.25), channel_id=1, source_target_pairs={{0,8},{8,16},{16,24},{24,32},{32,40},{40,48},{48,56},{56,64},{64,7... | collective-permute-start | bytes 24584 | tf_op jit(solution)/shard_map/ppermute | solution.py:19
  60.4 228.9 %collective-permute-start.3 = (f32[64,32]{0,1:T(8,128)S(1)}, f32[64,32]{0,1:T(8,128)S(1)}, u32[]{:S(2)}, u32[]{:S(2)}) collective-permute-start(f32[64,32]{0,1:T(8,128)S(1)} %get-tuple-element.26), channel_id=1, source_target_pairs={{8,0},{16,8},{24,16},{32,24},{40,32},{48,40},{56,48},{64,56},{72,6... | collective-permute-start | bytes 24584 | tf_op jit(solution)/shard_map/ppermute | solution.py:20
  289.5 43.2 %copy-start.4 = (f32[64,128]{1,0:T(8,128)S(1)}, f32[64,128]{1,0:T(8,128)}, u32[]{:S(2)}) copy-start(f32[64,128]{1,0:T(8,128)} %param.13) | copy-start | bytes 98308
  309.3 10.5 collective-permute-start.4
  317.9 5.2 collective-permute-start.5
  323.5 121.1 %copy-start.1 = (bf16[64,64,128]{2,1,0:T(8,128)(2,1)S(1)}, bf16[64,64,128]{2,1,0:T(8,128)(2,1)}, u32[]{:S(2)}) copy-start(bf16[64,64,128]{2,1,0:T(8,128)(2,1)} %param.17) | copy-start | bytes 3145732
  327.7 355.1 %copy-start.12 = (s32[64]{0:T(128)S(1)}, s32[64]{0:T(128)}, u32[]{:S(2)}) copy-start(s32[64]{0:T(128)} %copy-done.11) | copy-start | bytes 772
  430.9 14.1 %collective-permute-start.6 = (f32[64,32]{0,1:T(8,128)S(1)}, f32[64,32]{0,1:T(8,128)S(1)}, u32[]{:S(2)}, u32[]{:S(2)}) collective-permute-start(f32[64,32]{0,1:T(8,128)S(1)} %get-tuple-element.21), channel_id=1, source_target_pairs={{0,8},{8,16},{16,24},{24,32},{32,40},{40,48},{48,56},{56,64},{64,7... | collective-permute-start | bytes 24584 | tf_op jit(solution)/shard_map/ppermute | solution.py:19
  440.3 5.1 collective-permute-start.7
  444.0 0.6 copy-start.10
  444.6 705.7 %all-reduce.12.cloned.1.call-start = ((), (), s32[]{:S(2)}) async-start(), calls=%async_computation.2 | async-start | bytes 131072
  447.5 235.3 %collective-permute-start.8 = (f32[64,32]{0,1:T(8,128)S(1)}, f32[64,32]{0,1:T(8,128)S(1)}, u32[]{:S(2)}, u32[]{:S(2)}) collective-permute-start(f32[64,32]{0,1:T(8,128)S(1)} %get-tuple-element.19), channel_id=1, source_target_pairs={{0,8},{8,16},{16,24},{24,32},{32,40},{40,48},{48,56},{56,64},{64,7... | collective-permute-start | bytes 24584 | tf_op jit(solution)/shard_map/ppermute | solution.py:19
  450.8 232.0 %collective-permute-start.9 = (f32[64,32]{0,1:T(8,128)S(1)}, f32[64,32]{0,1:T(8,128)S(1)}, u32[]{:S(2)}, u32[]{:S(2)}) collective-permute-start(f32[64,32]{0,1:T(8,128)S(1)} %get-tuple-element.20), channel_id=1, source_target_pairs={{8,0},{16,8},{24,16},{32,24},{40,32},{48,40},{56,48},{64,56},{72,6... | collective-permute-start | bytes 24584 | tf_op jit(solution)/shard_map/ppermute | solution.py:20
  759.4 0.6 copy-start.5
  779.8 10.2 collective-permute-start.10
  788.1 5.2 collective-permute-start.11
  793.7 9.2 copy-start.6
  797.9 355.0 %copy-start.13 = (s32[64]{0:T(128)S(1)}, s32[64]{0:T(128)}, u32[]{:S(2)}) copy-start(s32[64]{0:T(128)} %copy-done.11) | copy-start | bytes 772
  882.1 348.0 %copy-start.7 = (f32[64,128]{1,0:T(8,128)}, f32[64,128]{1,0:T(8,128)S(1)}, u32[]{:S(2)}) copy-start(f32[64,128]{1,0:T(8,128)S(1)} %fusion.36) | copy-start | bytes 98308
  901.8 13.2 %collective-permute-start.12 = (f32[64,32]{0,1:T(8,128)S(1)}, f32[64,32]{0,1:T(8,128)S(1)}, u32[]{:S(2)}, u32[]{:S(2)}) collective-permute-start(f32[64,32]{0,1:T(8,128)S(1)} %get-tuple-element.15), channel_id=1, source_target_pairs={{0,8},{8,16},{16,24},{24,32},{32,40},{40,48},{48,56},{56,64},{64,7... | collective-permute-start | bytes 24584 | tf_op jit(solution)/shard_map/ppermute | solution.py:19
  910.3 5.1 collective-permute-start.13
  914.0 0.6 copy-start.8
  917.5 235.3 %collective-permute-start.14 = (f32[64,32]{0,1:T(8,128)S(1)}, f32[64,32]{0,1:T(8,128)S(1)}, u32[]{:S(2)}, u32[]{:S(2)}) collective-permute-start(f32[64,32]{0,1:T(8,128)S(1)} %get-tuple-element.13), channel_id=1, source_target_pairs={{0,8},{8,16},{16,24},{24,32},{32,40},{40,48},{48,56},{56,64},{64,7... | collective-permute-start | bytes 24584 | tf_op jit(solution)/shard_map/ppermute | solution.py:19
  920.9 232.0 %collective-permute-start.15 = (f32[64,32]{0,1:T(8,128)S(1)}, f32[64,32]{0,1:T(8,128)S(1)}, u32[]{:S(2)}, u32[]{:S(2)}) collective-permute-start(f32[64,32]{0,1:T(8,128)S(1)} %get-tuple-element.14), channel_id=1, source_target_pairs={{8,0},{16,8},{24,16},{32,24},{40,32},{48,40},{56,48},{64,56},{72,6... | collective-permute-start | bytes 24584 | tf_op jit(solution)/shard_map/ppermute | solution.py:20
Sparse Core Ops, SparseCore 0:
  49.5 237.2 all-reduce.7
  444.7 235.5 all-reduce.9
  914.8 235.4 all-reduce.11
where the time goes:
time: 1240 us
  waiting for transfers between devices  687 us (55%)
  blocking collectives  401 us (32%)
  starting transfers between devices  70.7 us (6%)
  local copies, waits for them, and re-layouts  22.2 us (2%)
  between operations  20.4 us (2%)
  other arithmetic  18.5 us (1%)
  matrix products  16.6 us (1%)
    unnamed x6, waiting for transfers between devices  680 us
    psum x4, blocking collectives, single_total(): return lax.psum(jnp.sum(first_vec * second_vec), ('slab', 'grp'))  302 us
    all_gather x5, blocking collectives, gather_slab(): return lax.all_gather(vector, 'grp', axis=1, tiled=True)  99 us
    ppermute x8, starting transfers between devices, padded_2(): before = lax.ppermute(last, axis, up)  54.8 us
  transfers between devices with their start and end apart: 19, of which 7 were waited for; matrix products, arithmetic and copies ran while one was open for 2% of the time, Pallas kernels for 0%

commit v1 on v0

v1 whole, which is shorter than its diff:
```python
import jax
import jax.numpy as jnp
from jax import lax
from jax.sharding import PartitionSpec as P

AXES = ("slab", "grp")
precise = lax.Precision.HIGHEST


def ein(pattern, *operands):
    return jnp.einsum(pattern, *operands, precision=precise, preferred_element_type=jnp.float32)


def local(
    right_side,
    stiffness,
    columns,
    margin_rows,
    local_inverse,
    margin_inverse,
    basis,
    coarse_counts,
    coarse_inverse,
):
    slabs, groups = lax.axis_size("slab"), lax.axis_size("grp")
    width = margin_rows.shape[2]
    size, rows = right_side.shape
    modes = basis.shape[0]
    group = lax.axis_index("grp")
    half = groups // 2
    is_low = group < half
    face_rows = jnp.where(is_low, margin_rows[0, 0], margin_rows[0, 1]) - group * rows
    select = (face_rows[:, None] == jnp.arange(rows, dtype=jnp.int32)[None, :]).astype(jnp.float32)
    live = (jnp.arange(modes, dtype=jnp.int32) < coarse_counts[0]).astype(jnp.float32)

    def pairs(low_step):
        found = []
        for s in range(slabs):
            for g in range(groups):
                other = s + (low_step if g < half else -low_step)
                if 0 <= other < slabs:
                    found.append((s * groups + g, other * groups + g))
        return found

    blocks = jnp.where(is_low, margin_inverse[:, :, width:], margin_inverse[:, :, :width])
    blocks = lax.ppermute(blocks.astype(jnp.float32), AXES, pairs(1))
    inverse = local_inverse.astype(jnp.float32) + ein("ijt,tb->ijb", blocks, select)

    def project(vector):
        return ein("jib,ib->j", basis, vector) * live

    def share(projected, dots):
        row = jnp.concatenate([projected, jnp.stack(dots)]) if dots else projected
        row = jnp.pad(row, (0, 128 - row.shape[0]))
        table = jnp.broadcast_to(row[None, :], (slabs * groups, 128))
        table = lax.all_to_all(table, AXES, 0, 0).reshape(slabs, groups, 128).sum(axis=1)
        totals = table[:, modes:].sum(axis=0)
        mine = lax.dynamic_index_in_dim(table, lax.axis_index("slab"), 0, keepdims=False)[:modes]
        weights = ein("jn,n->j", coarse_inverse, table[:, :modes].reshape(-1)) * live
        return mine, weights, totals

    def expand(weights):
        return ein("jib,j->ib", basis, weights)

    def solve_local(vector):
        return ein("ijb,jb->ib", inverse, vector)

    def stiff(vector):
        rim = lax.ppermute(ein("ib,tb->it", vector, select), AXES, pairs(-1))
        sent = jnp.concatenate([vector, rim], axis=1)
        sent = jnp.broadcast_to(sent[None], (groups,) + sent.shape)
        got = lax.all_to_all(sent, "grp", 0, 0)
        own = jnp.moveaxis(got[:, :, :rows], 0, 1).reshape(size, groups * rows)
        upper = got[:half, :, rows:].sum(axis=0)
        lower = got[half:, :, rows:].sum(axis=0)
        extended = jnp.concatenate([lower, own, upper], axis=1)
        return ein("kijb,jkb->ib", stiffness, jnp.take(extended, columns, axis=1))

    def dot(a, b):
        return jnp.sum(a * b)

    r0 = right_side
    p_r0, w_r0, _ = share(project(r0), [])
    z0 = solve_local(r0) + expand(w_r0)

    q0 = stiff(z0)
    p_q0, w_q0, t = share(project(q0), [dot(r0, z0), dot(z0, q0)])
    e0, z0q0 = t[0], t[1]
    m0 = solve_local(q0) + expand(w_q0)
    step0 = e0 / z0q0
    r1 = r0 - step0 * q0
    z1 = z0 - step0 * m0

    y1 = stiff(z1)
    s_y1 = solve_local(y1)
    dots = [dot(r1, z1), dot(z1, y1), dot(z1, q0), dot(z0, y1), dot(r1, s_y1), dot(y1, s_y1)]
    dots += [dot(q0, s_y1), dot(r1, m0), dot(y1, m0), dot(q0, m0)]
    p_y1, w_y1, t = share(project(y1), dots)
    e1, z1y1, z1q0, z0y1, r1s, y1s, q0s, r1m0, y1m0, q0m0 = (t[i] for i in range(len(dots)))
    beta0 = e1 / e0
    step1 = e1 / (z1y1 + beta0 * (z1q0 + z0y1) + beta0 * beta0 * z0q0)
    d1 = z1 + beta0 * z0
    q1 = y1 + beta0 * q0
    x2 = step0 * z0 + step1 * d1
    r2 = r1 - step1 * q1
    z2 = z1 - step1 * (s_y1 + expand(w_y1) + beta0 * m0)

    p_r1 = p_r0 - step0 * p_q0
    p_q1 = p_y1 + beta0 * p_q0
    coarse = jnp.sum((step1 * p_q1 - p_r1) * w_y1)
    coarse = jnp.broadcast_to(coarse, (slabs, 1, 128))
    coarse = lax.all_to_all(coarse, "slab", 0, 0).sum(axis=0)[0, 0]
    q1m1 = y1s + beta0 * (y1m0 + q0s) + beta0 * beta0 * q0m0
    e2 = e1 + step1 * (coarse + step1 * q1m1 - (z1y1 + beta0 * z1q0) - (r1s + beta0 * r1m0))
    return x2, r2, z2 + e2 / e1 * d1


def solution(mesh):
    in_specs = (
        P(None, AXES),
        P(None, None, None, AXES),
        P(None, AXES),
        P("slab", None, None),
        P(None, None, AXES),
        P(None, None, "slab"),
        P(None, None, AXES),
        P("slab"),
        P("slab", None),
    )
    out_specs = (P(None, AXES),) * 3
    return jax.shard_map(local, mesh=mesh, in_specs=in_specs, out_specs=out_specs, check_vma=False)
```

time: 1240 us -> 209 us (0.17)
  waiting for transfers between devices: 687 us -> 60.7 us
  blocking collectives: 401 us -> 19.2 us
  starting transfers between devices: 70.7 us -> 48.2 us
    unnamed x6 -> x0, waiting for transfers between devices: 680 us -> none
    psum x4 -> x0, blocking collectives: 302 us -> none  [single_total(): return lax.psum(jnp.sum(first_vec * second_vec), ('slab', 'grp'))]
    all_gather x5 -> x0, blocking collectives: 99 us -> none  [gather_slab(): return lax.all_gather(vector, 'grp', axis=1, tiled=True)]
    ppermute x16 -> x3, starting transfers between devices: 70.6 us -> 7.95 us  [the longest x2 4.42 us: stiff(): rim = lax.ppermute(ein('ib,tb->it', vector, select), AXES, pairs(-1))]
    all_to_all x0 -> x5, waiting for transfers between devices: none -> 47 us  [the longest x3 28 us: share(): lax.all_to_all(table, AXES, 0, 0).reshape(slabs, groups, 128).sum(axis=1)]
    all_to_all x0 -> x5, starting transfers between devices: none -> 40.3 us  [the longest x3 31.3 us: share(): lax.all_to_all(table, AXES, 0, 0).reshape(slabs, groups, 128).sum(axis=1)]
    all_to_all x0 -> x1, blocking collectives: none -> 19.2 us  [stiff(): got = lax.all_to_all(sent, 'grp', 0, 0)]
  transfers between devices with their start and end apart: 19 -> 8, of which waited for: 7 -> 8; matrix products, arithmetic and copies ran while one was open for 2% -> 5% of each run, Pallas kernels for 0% -> 0%
where the time goes in v1:
time: 209 us; the launch traced here: 208 us
  waiting for transfers between devices  60.7 us (29%)
  starting transfers between devices  48.2 us (23%)
  local copies, waits for them, and re-layouts  29 us (14%)
  other arithmetic  21.8 us (10%)
  blocking collectives  19.2 us (9%)
  matrix products  14.9 us (7%)
  between operations  13.7 us (7%)
    all_to_all x3, starting transfers between devices, share(): lax.all_to_all(table, AXES, 0, 0).reshape(slabs, groups, 128).sum(axis=1)  31.3 us
    all_to_all x3, waiting for transfers between devices, share(): lax.all_to_all(table, AXES, 0, 0).reshape(slabs, groups, 128).sum(axis=1)  28 us
    all_to_all x1, blocking collectives, stiff(): got = lax.all_to_all(sent, 'grp', 0, 0)  19.2 us
    all_to_all x1, waiting for transfers between devices, stiff(): got = lax.all_to_all(sent, 'grp', 0, 0)  18 us
    dot_general x12, matrix products, ein(): jnp.einsum(pattern, *operands, precision=precise, preferred_element_type=...  14.9 us
    dot_general x4, other arithmetic, ein(): jnp.einsum(pattern, *operands, precision=precise, preferred_element_type=...  10.7 us
    ppermute x1, waiting for transfers between devices, local(): blocks = lax.ppermute(blocks.astype(jnp.float32), AXES, pairs(1))  7.32 us
    ppermute x2, waiting for transfers between devices, stiff(): rim = lax.ppermute(ein('ib,tb->it', vector, select), AXES, pairs(-1))  6.37 us
  transfers between devices with their start and end apart: 8, of which 8 were waited for; matrix products, arithmetic and copies ran while one was open for 5% of the time, Pallas kernels for 0%

profile of v1, /device:TPU:1, one launch (start us, length us, event | category | flops | bytes accessed | tf_op | source)
XLA Modules:
  0.0 207.5 jit_solution(17275332940887910774)
XLA Ops:
  1.4 2.5 %fusion.2 = f32[64]{0:T(128)S(1)} fusion(f32[64,128,1]{1,2,0:T(1,128)} %bitcast.222, bf16[64,64,128]{2,1,0:T(8,128)(2,1)} %param.17, s32[]{:T(128)} %bitcast.207), kind=kOutput, calls=%fused_computation.13 | convolution fusion | flops 6291584 | bytes 1081604 | tf_op jit(solution)/shard_map/jib,ib->j/dot_general | solution.py:11
  3.9 0.7 broadcast_in_dim.21
  4.7 15.7 %all-to-all-start = ((f32[256,1,128]{2,1,0:T(1,128)}), f32[256,1,128]{2,1,0:T(1,128)S(1)}, u32[]{:S(2)}, u32[]{:S(2)}) async-start(f32[256,1,128]{2,1,0:T(1,128)} %broadcast_in_dim.21), calls=%async_computation | async-start | bytes 262144 | tf_op jit(solution)/shard_map/all_to_all | solution.py:56
  20.3 1.5 fusion.48
  21.8 1.6 copy.95
  23.4 1.2 copy.94
  24.6 2.1 %select_convert_fusion = f32[64,64,32]{1,2,0:T(8,128)} fusion(bf16[64,64,32]{1,2,0:T(8,128)(2,1)} %copy.94, bf16[64,64,32]{1,2,0:T(8,128)(2,1)S(1)} %copy.95, pred[]{:T(512)S(6)} %lt.23), kind=kLoop, calls=%fused_computation.26 | loop fusion | flops 262144 | bytes 1048577 | tf_op jit(solution)/shard_map/convert_element_type | solution.py:46
  26.7 3.5 %collective-permute-start = (f32[64,64,32]{1,2,0:T(8,128)}, f32[64,64,32]{1,2,0:T(8,128)S(1)}, u32[]{:S(2)}, u32[]{:S(2)}) collective-permute-start(f32[64,64,32]{1,2,0:T(8,128)} %select_convert_fusion), channel_id=1, source_target_pairs={{0,8},{1,9},{2,10},{3,11},{8,16},{9,17},{10,18},{11,19},{12,4},{13... | collective-permute-start | bytes 1572872 | tf_op jit(solution)/shard_map/ppermute | solution.py:46
  30.3 3.0 %all-to-all-done = f32[256,1,128]{2,1,0:T(1,128)S(1)} async-done(((f32[256,1,128]{2,1,0:T(1,128)}), f32[256,1,128]{2,1,0:T(1,128)S(1)}, u32[]{:S(2)}, u32[]{:S(2)}) %all-to-all-start) | async-done | bytes 131104 | tf_op jit(solution)/shard_map/all_to_all | solution.py:56
  34.0 1.0 fusion.16
  35.0 7.3 %collective-permute-done = f32[64,64,32]{1,2,0:T(8,128)S(1)} collective-permute-done((f32[64,64,32]{1,2,0:T(8,128)}, f32[64,64,32]{1,2,0:T(8,128)S(1)}, u32[]{:S(2)}, u32[]{:S(2)}) %collective-permute-start) | collective-permute-done | bytes 524320 | tf_op jit(solution)/shard_map/ppermute | solution.py:46
  42.3 1.0 copy-done.7
  43.3 3.1 %multiply_reduce_fusion.2 = (f32[128,64]{0,1:T(8,128)S(1)}, f32[64,64,128]{2,1,0:T(8,128)S(1)}) fusion(f32[128,64]{0,1:T(8,128)S(1)} %bitcast.223, f32[64,64,32]{1,2,0:T(8,128)} %copy-done.7, s32[32]{0:T(128)S(1)} %fusion.44, bf16[64,64,128]{2,1,0:T(8,128)(2,1)S(1)} %copy-done.6), kind=kOutput, calls=%fused_computation.8 | convolution fusion | flops 203419648 | bytes 3735680 | tf_op jit(solution)/shard_map/ijt,tb->ijb/dot_general | solution.py:11
  46.6 1.9 collective-permute-start.1
  48.6 3.8 %collective-permute-done.1 = f32[64,32]{0,1:T(8,128)S(1)} collective-permute-done((f32[64,32]{0,1:T(8,128)S(1)}, f32[64,32]{0,1:T(8,128)S(1)}, u32[]{:S(2)}, u32[]{:S(2)}) %collective-permute-start.1) | collective-permute-done | bytes 8224 | tf_op jit(solution)/shard_map/ppermute | solution.py:69
  52.4 0.8 broadcast_in_dim.22
  53.3 4.9 %all-to-all-start.1 = ((f32[8,64,160]{2,1,0:T(8,128)}), f32[8,64,160]{2,1,0:T(8,128)S(1)}, u32[]{:S(2)}, u32[]{:S(2)}) async-start(f32[8,64,160]{2,1,0:T(8,128)} %broadcast_in_dim.22), calls=%async_computation.1 | async-start | bytes 1048576 | tf_op jit(solution)/shard_map/all_to_all | solution.py:72
  58.3 18.0 %all-to-all-done.1 = f32[8,64,160]{2,1,0:T(8,128)S(1)} async-done(((f32[8,64,160]{2,1,0:T(8,128)}), f32[8,64,160]{2,1,0:T(8,128)S(1)}, u32[]{:S(2)}, u32[]{:S(2)}) %all-to-all-start.1) | async-done | bytes 327712 | tf_op jit(solution)/shard_map/all_to_all | solution.py:72
  76.5 1.0 copy.47
  77.5 1.1 pad_maximum_fusion
  78.5 2.8 %gather_fusion = f32[896,64]{1,0:T(8,128)} fusion(f32[64,1088]{0,1:T(8,128)S(1)} %pad_maximum_fusion, s32[1024]{0:T(1024)S(1)} %pad_clamp_fusion), kind=kCustom, calls=%fused_computation.clone | custom fusion | bytes 462336 | tf_op jit(solution)/shard_map/jit(_take)/gather | solution.py:77
  81.3 1.2 select_bitcast_fusion.1
  82.7 5.1 %fusion = f32[128,64]{0,1:T(8,128)S(1)} fusion(f32[128,64,7]{0,1,2:T(8,128)S(1)} %copy.97, bf16[7,64,64,128]{3,2,1,0:T(8,128)(2,1)} %param.12), kind=kLoop, calls=%fused_computation.4 | loop fusion | flops 11001856 | bytes 7602176 | tf_op jit(solution)/shard_map/kijb,jkb->ib/dot_general | solution.py:11
  88.4 1.3 fusion.3
  89.7 1.4 select_maximum_fusion
  91.8 9.4 %all-to-all-start.2 = ((f32[256,1,128]{2,1,0:T(1,128)}), f32[256,1,128]{2,1,0:T(1,128)S(1)}, u32[]{:S(2)}, u32[]{:S(2)}) async-start(f32[256,1,128]{2,1,0:T(1,128)} %broadcast_in_dim.23), calls=%async_computation.2 | async-start | bytes 262144 | tf_op jit(solution)/shard_map/all_to_all | solution.py:56
  101.5 12.7 %all-to-all-done.2 = f32[256,1,128]{2,1,0:T(1,128)S(1)} async-done(((f32[256,1,128]{2,1,0:T(1,128)}), f32[256,1,128]{2,1,0:T(1,128)S(1)}, u32[]{:S(2)}, u32[]{:S(2)}) %all-to-all-start.2) | async-done | bytes 131104 | tf_op jit(solution)/shard_map/all_to_all | solution.py:56
  115.5 2.2 %fusion.13 = f32[1,64,128]{2,0,1:T(1,128)S(1)} fusion(f32[64,1,1]{0,1,2:T(1,128)S(1)} %fusion.7, bf16[64,64,128]{2,1,0:T(8,128)(2,1)} %param.17), kind=kOutput, calls=%fused_computation.32 | convolution fusion | flops 6291456 | bytes 1081600 | tf_op jit(solution)/shard_map/jib,j->ib/dot_general | solution.py:11
  119.7 2.5 %collective-permute-start.2 = (f32[64,32]{0,1:T(8,128)S(1)}, f32[64,32]{0,1:T(8,128)S(1)}, u32[]{:S(2)}, u32[]{:S(2)}) collective-permute-start(f32[64,32]{0,1:T(8,128)S(1)} %fusion.35), channel_id=1, source_target_pairs={{4,12},{5,13},{6,14},{7,15},{8,0},{9,1},{10,2},{11,3},{12,20},{13,... | collective-permute-start | bytes 24584 | tf_op jit(solution)/shard_map/ppermute | solution.py:69
  122.2 2.6 %collective-permute-done.2 = f32[64,32]{0,1:T(8,128)S(1)} collective-permute-done((f32[64,32]{0,1:T(8,128)S(1)}, f32[64,32]{0,1:T(8,128)S(1)}, u32[]{:S(2)}, u32[]{:S(2)}) %collective-permute-start.2) | collective-permute-done | bytes 8224 | tf_op jit(solution)/shard_map/ppermute | solution.py:69
  125.0 19.2 %all_to_all.33 = f32[8,64,160]{2,1,0:T(8,128)S(1)} all-to-all(f32[8,64,160]{2,1,0:T(8,128)S(1)} %broadcast_in_dim.24), channel_id=1, replica_groups=mesh['slab'=32,'grp'=8] {'grp'}, dimensions={0} | all-to-all | bytes 655360 | tf_op jit(solution)/shard_map/all_to_all | solution.py:72
  145.5 1.0 copy.51
  146.5 1.1 pad_maximum_fusion.1
  147.6 3.0 %gather_fusion.1 = f32[896,64]{1,0:T(8,128)} fusion(f32[64,1088]{0,1:T(8,128)S(1)} %pad_maximum_fusion.1, s32[1024]{0:T(1024)} %copy-done.12), kind=kCustom, calls=%fused_computation.1.clone | custom fusion | bytes 462336 | tf_op jit(solution)/shard_map/jit(_take)/gather | solution.py:77
  150.7 1.2 select_bitcast_fusion
  152.1 5.0 %fusion.1 = f32[128,64]{0,1:T(8,128)S(1)} fusion(f32[128,64,7]{0,1,2:T(8,128)S(1)} %copy.101, bf16[7,64,64,128]{3,2,1,0:T(8,128)(2,1)} %param.12), kind=kLoop, calls=%fused_computation.5 | loop fusion | flops 11001856 | bytes 7602176 | tf_op jit(solution)/shard_map/kijb,jkb->ib/dot_general | solution.py:11
  157.5 0.8 copy-done.3
  158.3 1.3 fusion.4
  159.6 0.7 fusion.31
  160.3 6.4 %concatenate.23 = f32[74]{0:T(128)S(1)} concatenate(f32[64]{0:T(128)S(1)} %fusion.4, f32[1]{0:T(128)} %bitcast.53, f32[1]{0:T(128)} %bitcast.54, f32[1]{0:T(128)} %bitcast.55, f32[1]{0:T(128)} %bitcast.56, f32[1]{0:T(128)} %bitcast.59, f32[1]{0:T(128)} %bitcast.60, f32[1]{0:T(128)} %bitcast.61, f32[1]{0:T(128)} %bitcast.62, f32[1]{0:T(128)} %bitcast.63, f32[1]{0:T(128)} %bitcast.64), dimensions={0} | concatenate | bytes 592 | tf_op jit(solution)/shard_map/concatenate | solution.py:53
  166.7 0.7 broadcast_in_dim.25
  167.4 6.3 %all-to-all-start.4 = ((f32[256,1,128]{2,1,0:T(1,128)}), f32[256,1,128]{2,1,0:T(1,128)S(1)}, u32[]{:S(2)}, u32[]{:S(2)}) async-start(f32[256,1,128]{2,1,0:T(1,128)} %broadcast_in_dim.25), calls=%async_computation.4 | async-start | bytes 262144 | tf_op jit(solution)/shard_map/all_to_all | solution.py:56
  174.4 12.3 %all-to-all-done.4 = f32[256,1,128]{2,1,0:T(1,128)S(1)} async-done(((f32[256,1,128]{2,1,0:T(1,128)}), f32[256,1,128]{2,1,0:T(1,128)S(1)}, u32[]{:S(2)}, u32[]{:S(2)}) %all-to-all-start.4) | async-done | bytes 131104 | tf_op jit(solution)/shard_map/all_to_all | solution.py:56
  192.0 1.2 fusion.45
  193.2 1.3 broadcast_in_dim.26
  194.5 4.0 %all-to-all-start.5 = ((f32[32,1,128]{2,1,0:T(1,128)}), f32[32,1,128]{2,1,0:T(1,128)S(1)}, u32[]{:S(2)}, u32[]{:S(2)}) async-start(f32[32,1,128]{2,1,0:T(1,128)} %broadcast_in_dim.26), calls=%async_computation.5 | async-start | bytes 32768 | tf_op jit(solution)/shard_map/all_to_all | solution.py:112
  198.5 1.0 fusion.10
  204.5 1.0 all-to-all-done.5
  (82 shorter events, 9.5 us)
Async XLA Ops:
  0.6 32.8 %copy-start = (f32[64,2048]{1,0:T(8,128)S(1)}, f32[64,2048]{1,0:T(8,128)}, u32[]{:S(2)}) copy-start(f32[64,2048]{1,0:T(8,128)} %param.19) | copy-start | bytes 1572868
  0.6 19.7 %copy-start.5 = (bf16[64,64,64]{2,1,0:T(8,128)(2,1)S(1)}, bf16[64,64,64]{2,1,0:T(8,128)(2,1)}, u32[]{:S(2)}) copy-start(bf16[64,64,64]{2,1,0:T(8,128)(2,1)} %param.16) | copy-start | bytes 1572868
  4.7 28.7 %all-to-all-start = ((f32[256,1,128]{2,1,0:T(1,128)}), f32[256,1,128]{2,1,0:T(1,128)S(1)}, u32[]{:S(2)}, u32[]{:S(2)}) async-start(f32[256,1,128]{2,1,0:T(1,128)} %broadcast_in_dim.21), calls=%async_computation | async-start | bytes 262144 | tf_op jit(solution)/shard_map/all_to_all | solution.py:56
  23.4 6.8 %copy-start.18 = (s32[1,2,32]{2,1,0:T(2,128)S(1)}, s32[1,2,32]{2,1,0:T(2,128)}, u32[]{:S(2)}) copy-start(s32[1,2,32]{2,1,0:T(2,128)} %param.14) | copy-start | bytes 772
  23.4 10.6 %copy-start.1 = (bf16[64,64,128]{2,1,0:T(8,128)(2,1)S(1)}, bf16[64,64,128]{2,1,0:T(8,128)(2,1)}, u32[]{:S(2)}) copy-start(bf16[64,64,128]{2,1,0:T(8,128)(2,1)} %param.17) | copy-start | bytes 3145732
  24.6 18.7 %copy-start.8 = (f32[64,128]{1,0:T(8,128)S(1)}, f32[64,128]{1,0:T(8,128)}, u32[]{:S(2)}) copy-start(f32[64,128]{1,0:T(8,128)} %param.11) | copy-start | bytes 98308
  26.7 15.6 %collective-permute-start = (f32[64,64,32]{1,2,0:T(8,128)}, f32[64,64,32]{1,2,0:T(8,128)S(1)}, u32[]{:S(2)}, u32[]{:S(2)}) collective-permute-start(f32[64,64,32]{1,2,0:T(8,128)} %select_convert_fusion), channel_id=1, source_target_pairs={{0,8},{1,9},{2,10},{3,11},{8,16},{9,17},{10,18},{11,19},{12,4},{13... | collective-permute-start | bytes 1572872 | tf_op jit(solution)/shard_map/ppermute | solution.py:46
  30.3 16.2 %copy-start.16 = (s32[32]{0:T(128)}, s32[32]{0:T(128)S(1)}, u32[]{:S(2)}) copy-start(s32[32]{0:T(128)S(1)} %fusion.44) | copy-start | bytes 388
  33.4 13.0 %copy-start.11 = (f32[32,128]{1,0:T(8,128)}, f32[32,128]{1,0:T(8,128)S(1)}, u32[]{:S(2)}) copy-start(f32[32,128]{1,0:T(8,128)S(1)} %bitcast_reduce_fusion.2) | copy-start | bytes 49156
  33.5 9.8 %copy-start.6 = (bf16[64,64,128]{2,1,0:T(8,128)(2,1)S(1)}, bf16[64,64,128]{2,1,0:T(8,128)(2,1)}, u32[]{:S(2)}) copy-start(bf16[64,64,128]{2,1,0:T(8,128)(2,1)} %param.15) | copy-start | bytes 3145732
  42.3 1.0 copy-start.7
  43.3 14.9 %copy-start.13 = (s32[7,128]{1,0:T(8,128)S(1)}, s32[7,128]{1,0:T(8,128)}, u32[]{:S(2)}) copy-start(s32[7,128]{1,0:T(8,128)} %param.13) | copy-start | bytes 10756
  46.6 5.7 %collective-permute-start.1 = (f32[64,32]{0,1:T(8,128)S(1)}, f32[64,32]{0,1:T(8,128)S(1)}, u32[]{:S(2)}, u32[]{:S(2)}) collective-permute-start(f32[64,32]{0,1:T(8,128)S(1)} %fusion.36), channel_id=1, source_target_pairs={{4,12},{5,13},{6,14},{7,15},{8,0},{9,1},{10,2},{11,3},{12,20},{13,... | collective-permute-start | bytes 24584 | tf_op jit(solution)/shard_map/ppermute | solution.py:69
  53.3 23.0 %all-to-all-start.1 = ((f32[8,64,160]{2,1,0:T(8,128)}), f32[8,64,160]{2,1,0:T(8,128)S(1)}, u32[]{:S(2)}, u32[]{:S(2)}) async-start(f32[8,64,160]{2,1,0:T(8,128)} %broadcast_in_dim.22), calls=%async_computation.1 | async-start | bytes 1048576 | tf_op jit(solution)/shard_map/all_to_all | solution.py:72
  58.2 23.1 %copy-start.12 = (s32[1024]{0:T(1024)}, s32[1024]{0:T(1024)S(1)}, u32[]{:S(2)}) copy-start(s32[1024]{0:T(1024)S(1)} %pad_clamp_fusion) | copy-start | bytes 12292
  58.3 23.1 %copy-start.14 = (pred[7,128]{1,0:T(8,128)(4,1)}, pred[7,128]{1,0:T(8,128)(4,1)S(1)}, u32[]{:S(2)}) copy-start(pred[7,128]{1,0:T(8,128)(4,1)S(1)} %compare_and_fusion) | copy-start | bytes 2692
  82.7 5.7 %copy-start.2 = (bf16[64,64,128]{2,1,0:T(8,128)(2,1)S(1)}, bf16[64,64,128]{2,1,0:T(8,128)(2,1)}, u32[]{:S(2)}) copy-start(bf16[64,64,128]{2,1,0:T(8,128)(2,1)} %param.17) | copy-start | bytes 3145732
  91.8 22.4 %all-to-all-start.2 = ((f32[256,1,128]{2,1,0:T(1,128)}), f32[256,1,128]{2,1,0:T(1,128)S(1)}, u32[]{:S(2)}, u32[]{:S(2)}) async-start(f32[256,1,128]{2,1,0:T(1,128)} %broadcast_in_dim.23), calls=%async_computation.2 | async-start | bytes 262144 | tf_op jit(solution)/shard_map/all_to_all | solution.py:56
  101.2 18.4 %copy-start.17 = (s32[32]{0:T(128)S(1)}, s32[32]{0:T(128)}, u32[]{:S(2)}) copy-start(s32[32]{0:T(128)} %copy-done.16) | copy-start | bytes 388
  119.7 5.1 %collective-permute-start.2 = (f32[64,32]{0,1:T(8,128)S(1)}, f32[64,32]{0,1:T(8,128)S(1)}, u32[]{:S(2)}, u32[]{:S(2)}) collective-permute-start(f32[64,32]{0,1:T(8,128)S(1)} %fusion.35), channel_id=1, source_target_pairs={{4,12},{5,13},{6,14},{7,15},{8,0},{9,1},{10,2},{11,3},{12,20},{13,... | collective-permute-start | bytes 24584 | tf_op jit(solution)/shard_map/ppermute | solution.py:69
  146.5 4.2 %copy-start.15 = (pred[7,128]{1,0:T(8,128)(4,1)S(1)}, pred[7,128]{1,0:T(8,128)(4,1)}, u32[]{:S(2)}) copy-start(pred[7,128]{1,0:T(8,128)(4,1)} %copy-done.14) | copy-start | bytes 2692
  157.1 1.2 copy-start.3
  157.1 2.5 %copy-start.9 = (f32[64,128]{1,0:T(8,128)S(1)}, f32[64,128]{1,0:T(8,128)}, u32[]{:S(2)}) copy-start(f32[64,128]{1,0:T(8,128)} %param.11) | copy-start | bytes 98308
  157.1 2.5 %copy-start.10 = (f32[64,128]{1,0:T(8,128)S(1)}, f32[64,128]{1,0:T(8,128)}, u32[]{:S(2)}) copy-start(f32[64,128]{1,0:T(8,128)} %get-tuple-element.22) | copy-start | bytes 98308
  157.5 41.1 %copy-start.4 = (bf16[64,64,128]{2,1,0:T(8,128)(2,1)S(1)}, bf16[64,64,128]{2,1,0:T(8,128)(2,1)}, u32[]{:S(2)}) copy-start(bf16[64,64,128]{2,1,0:T(8,128)(2,1)} %param.17) | copy-start | bytes 3145732
  167.4 19.3 %all-to-all-start.4 = ((f32[256,1,128]{2,1,0:T(1,128)}), f32[256,1,128]{2,1,0:T(1,128)S(1)}, u32[]{:S(2)}, u32[]{:S(2)}) async-start(f32[256,1,128]{2,1,0:T(1,128)} %broadcast_in_dim.25), calls=%async_computation.4 | async-start | bytes 262144 | tf_op jit(solution)/shard_map/all_to_all | solution.py:56
  194.5 11.0 %all-to-all-start.5 = ((f32[32,1,128]{2,1,0:T(1,128)}), f32[32,1,128]{2,1,0:T(1,128)S(1)}, u32[]{:S(2)}, u32[]{:S(2)}) async-start(f32[32,1,128]{2,1,0:T(1,128)} %broadcast_in_dim.26), calls=%async_computation.5 | async-start | bytes 32768 | tf_op jit(solution)/shard_map/all_to_all | solution.py:112

commit v2 on v1

v2 whole, which is shorter than its diff:
```python
import functools

import jax
import jax.numpy as jnp
from jax import lax
from jax.experimental import pallas as pl
from jax.experimental.pallas import tpu as pltpu
from jax.sharding import PartitionSpec as P

AXES = ("slab", "grp")
F32, I32 = jnp.float32, jnp.int32
LANES = 128
VMEM = pl.BlockSpec(memory_space=pltpu.VMEM)
SMEM = pl.BlockSpec(memory_space=pltpu.SMEM)
precise = lax.Precision.HIGHEST


def call(body, outs, specs, *operands, scratch=(), flops=0, **static):
    shapes = [jax.ShapeDtypeStruct(shape, dtype) for shape, dtype in outs]
    read = sum(x.size * x.dtype.itemsize for x in operands)
    return pl.pallas_call(
        functools.partial(body, **static),
        out_shape=shapes,
        in_specs=specs,
        out_specs=[VMEM] * len(shapes),
        scratch_shapes=list(scratch),
        cost_estimate=pl.CostEstimate(flops=flops, bytes_accessed=read, transcendentals=0),
    )(*operands)


def tile_sum(parts):
    return jnp.concatenate([jnp.sum(part, axis=0, keepdims=True) for part in parts], axis=0)


def lane_index(rows=8):
    return lax.broadcasted_iota(I32, (rows, LANES), 1)


def pick_lanes(block, index):
    index = jnp.broadcast_to(index, block.shape)
    return jnp.take_along_axis(block, index, axis=1, mode="promise_in_bounds")


def total(a, b):
    return jnp.sum(a * b, axis=0, keepdims=True)


def project_into(sums_ref, basis_ref, vector):
    modes, size, _ = basis_ref.shape

    def eight(step, carry):
        first = pl.multiple_of(step * 8, 8)
        parts = []
        for r in range(8):
            acc = jnp.zeros((16, LANES), F32)
            for t in range(0, size, 16):
                acc += basis_ref[first + r, t : t + 16, :].astype(F32) * vector[t : t + 16]
            parts.append(acc)
        sums_ref[pl.ds(first, 8), :] = tile_sum(parts)
        return carry

    lax.fori_loop(0, modes // 8, eight, 0)


def block_product(out_ref, blocks_ref, vector):
    size = blocks_ref.shape[0]

    def eight(step, carry):
        first = pl.multiple_of(step * 8, 8)
        parts = []
        for r in range(8):
            acc = jnp.zeros((8, LANES), F32)
            for t in range(0, size, 8):
                acc += blocks_ref[first + r, t : t + 8, :] * vector[t : t + 8]
            parts.append(acc)
        out_ref[pl.ds(first, 8), :] = tile_sum(parts)
        return carry

    lax.fori_loop(0, size // 8, eight, 0)


def write_table(table_ref, sums_ref, count, modes, dots):
    rest = LANES - modes
    rows = dots + [jnp.zeros((1, LANES), F32)] * (rest - len(dots))
    sums_ref[modes:, :] = jnp.concatenate(rows, axis=0)
    row = lax.dot_general(
        jnp.ones((8, LANES), F32),
        sums_ref[...],
        (((1,), (1,)), ((), ())),
        precision=precise,
        preferred_element_type=F32,
    )
    lane = lane_index()
    row = jnp.where((lane < count) | (lane >= modes), row, 0.0)
    for m in range(table_ref.shape[0] // 8):
        table_ref[8 * m : 8 * m + 8, :] = row


def begin_body(
    place, margin_rows, counts, field, basis, margin, table, packed, meta, sums, *, groups, rows
):
    size = field.shape[0]
    width = margin_rows.shape[2]
    group = place[0]
    face = jnp.where(group < groups // 2, 0, 1)
    project_into(sums, basis, field[...])
    write_table(table, sums, counts[0], basis.shape[0], [])

    lane = lane_index(1)
    slot, owned = jnp.zeros((1, LANES), I32), jnp.zeros((1, LANES), I32)
    source = jnp.full((1, LANES), -1, I32)
    for t in range(width):
        row = margin_rows[0, face, t] - group * rows
        hit = lane == row
        slot = jnp.where(hit, t, slot)
        owned = jnp.where(hit, 1, owned)
        source = jnp.where(lane % width == t, row, source)
    inside = ((source >= 0) & (source < rows)).astype(I32)
    source = jnp.clip(source, 0, rows - 1)
    meta[...] = jnp.concatenate([slot, owned, source, inside, jnp.zeros((4, LANES), I32)], axis=0)

    parts = LANES // width
    depth = size // parts
    lanes = lane_index(depth)
    full = LANES // margin.shape[2]

    def one(i, carry):
        result = jnp.zeros((depth, LANES), F32)
        for a in range(parts):
            block = margin[i, a * depth : (a + 1) * depth, :].astype(F32)
            block = jnp.concatenate([block] * full, axis=1)
            upper = pltpu.roll(block, (a * width - width) % LANES, 1)
            lower = pltpu.roll(block, a * width, 1)
            part = jnp.where(face == 0, upper, lower)
            result = jnp.where((lanes >= a * width) & (lanes < (a + 1) * width), part, result)
        packed[i] = result
        return carry

    lax.fori_loop(0, size, one, 0, unroll=4)


def inverse_body(meta, local_inverse, packed, field, inverse, solved, *, width):
    size, depth, _ = packed.shape
    slot = meta[0:1, :]
    owned = jnp.broadcast_to(meta[1:2, :], (depth, LANES)) > 0

    def one(i, carry):
        block = packed[i]
        for a in range(size // depth):
            extra = jnp.where(owned, pick_lanes(block, slot + a * width), 0.0)
            own = local_inverse[i, a * depth : (a + 1) * depth, :].astype(F32)
            inverse[i, a * depth : (a + 1) * depth, :] = own + extra
        return carry

    lax.fori_loop(0, size, one, 0, unroll=4)
    block_product(solved, inverse, field[...])


def coarse_weights(weights_ref, table, coarse, count):
    modes = coarse.shape[0]
    lane = lane_index()
    accs = [jnp.zeros((8, LANES), F32) for _ in range(modes // 8)]
    totals = jnp.zeros((8, LANES), F32)
    for m in range(table.shape[0] // 16):
        even, odd = table[16 * m : 16 * m + 8, :], table[16 * m + 8 : 16 * m + 16, :]
        totals += even + odd
        both = jnp.where(lane < modes, even, pltpu.roll(odd, modes, 1))
        both = jnp.sum(both, axis=0, keepdims=True)
        for r in range(modes // 8):
            accs[r] += coarse[8 * r : 8 * r + 8, LANES * m : LANES * m + LANES] * both
    weights = jnp.dot(
        jnp.concatenate(accs, axis=0),
        jnp.ones((LANES, LANES), F32),
        precision=precise,
        preferred_element_type=F32,
    )
    rows = lax.broadcasted_iota(I32, (modes, LANES), 0)
    weights_ref[...] = jnp.where(rows < count, weights, 0.0)
    return jnp.sum(totals, axis=0, keepdims=True)


def expand(weights_ref, basis):
    modes, size, _ = basis.shape

    def eight(step, accs):
        first = pl.multiple_of(step * 8, 8)
        weights = weights_ref[pl.ds(first, 8), :]
        accs = list(accs)
        for r in range(8):
            weight = weights[r : r + 1, :]
            for t in range(size // 16):
                accs[t] += basis[first + r, 16 * t : 16 * t + 16, :].astype(F32) * weight
        return tuple(accs)

    accs = tuple(jnp.zeros((16, LANES), F32) for _ in range(size // 16))
    return jnp.concatenate(lax.fori_loop(0, modes // 8, eight, accs), axis=0)


def own_row(table, slab):
    return jnp.sum(table[pl.ds(pl.multiple_of(slab * 8, 8), 8), :], axis=0, keepdims=True)


def spread(row, lane):
    return jnp.broadcast_to(row[:, lane : lane + 1], (1, LANES))


def send_out(vector, meta, rim, send, *, width):
    size = vector.shape[0]
    depth = rim.shape[0]
    picked = pick_lanes(vector, meta[2:3, :])
    picked = jnp.where(jnp.broadcast_to(meta[3:4, :], picked.shape) > 0, picked, 0.0)
    lanes = lane_index(depth)
    result = jnp.zeros((depth, LANES), F32)
    for a in range(size // depth):
        part = picked[a * depth : (a + 1) * depth]
        result = jnp.where((lanes >= a * width) & (lanes < (a + 1) * width), part, result)
    rim[...] = result
    for g in range(send.shape[0]):
        send[g, :size, :] = vector
        send[g, size:, :] = result


def first_body(
    place, counts, table, coarse, basis, solved, meta, search, mine, rim, send, weights, *, width
):
    coarse_weights(weights, table, coarse, counts[0])
    mine[...] = jnp.broadcast_to(own_row(table, place[1]), (8, LANES))
    search[...] = solved[...] + expand(weights, basis)
    send_out(search[...], meta, rim, send, width=width)


def second_body(
    place,
    counts,
    table,
    coarse,
    basis,
    solved,
    meta,
    field,
    search,
    image,
    mine0,
    answer,
    residual,
    search1,
    mine,
    scalars,
    rim,
    send,
    weights,
    *,
    width,
):
    modes = basis.shape[0]
    totals = coarse_weights(weights, table, coarse, counts[0])
    energy, curve = spread(totals, modes), spread(totals, modes + 1)
    step = energy / curve
    p_q0 = own_row(table, place[1])
    p_r1 = mine0[0:1, :] - step * p_q0
    mine[...] = jnp.concatenate([p_r1, p_q0, jnp.zeros((6, LANES), F32)], axis=0)
    scalars[...] = jnp.concatenate([energy, curve, step, jnp.zeros((5, LANES), F32)], axis=0)
    answer[...] = solved[...] + expand(weights, basis)
    residual[...] = field[...] - step * image[...]
    search1[...] = search[...] - step * answer[...]
    send_out(search1[...], meta, rim, send, width=width)


def pick_columns(got, columns, own, picked, width):
    groups, _, _ = got.shape
    size = own.shape[0]
    rows = LANES
    depth = got.shape[1] - size
    half = groups // 2
    upper = sum(got[g, size:, :] for g in range(half))
    lower = sum(got[g, size:, :] for g in range(half, groups))
    lanes = lane_index(depth)
    rims = []
    for a in range(size // depth):
        low = pltpu.roll(lower, (-a * width) % LANES, 1)
        high = pltpu.roll(upper, (width - a * width) % LANES, 1)
        rims.append(jnp.where(lanes < width, low, high))
    rims = jnp.concatenate(rims, axis=0)
    picked[0] = own[...]
    for k in range(1, columns.shape[0]):
        named = columns[k : k + 1, :] - width
        block = named // rows
        lane = named - block * rows
        inside = (named >= 0) & (named < groups * rows)
        rim_lane = jnp.where(named < 0, named + width, named - groups * rows + width)
        lane = jnp.where(inside, lane, rim_lane)
        block = jnp.broadcast_to(jnp.where(inside, block, groups), (8, LANES))
        lane = jnp.broadcast_to(lane, (8, LANES))
        for t in range(0, size, 8):
            value = pick_lanes(rims[t : t + 8], lane)
            for g in range(groups):
                value = jnp.where(block == g, pick_lanes(got[g, t : t + 8, :], lane), value)
            picked[k, t : t + 8, :] = value


def stiff_into(out_ref, stiffness, picked):
    entries, size, _, _ = stiffness.shape

    def eight(step, carry):
        first = pl.multiple_of(step * 8, 8)
        accs = [jnp.zeros((16, LANES), F32) for _ in range(8)]
        for k in range(entries):
            for t in range(0, size, 16):
                value = picked[k, t : t + 16, :]
                for r in range(8):
                    accs[r] += stiffness[k, first + r, t : t + 16, :].astype(F32) * value
        out_ref[pl.ds(first, 8), :] = tile_sum(accs)
        return carry

    lax.fori_loop(0, size // 8, eight, 0)


def stiff_body(counts, got, columns, stiffness, basis, inverse, *refs, others, pairs, width):
    vectors = refs[:others]
    image, solved, table, picked, sums = refs[others:]
    pick_columns(got, columns, vectors[0], picked, width)
    stiff_into(image, stiffness, picked)
    project_into(sums, basis, image[...])
    block_product(solved, inverse, image[...])
    named = list(vectors) + [image, solved]
    dots = [total(named[a][...], named[b][...]) for a, b in pairs]
    write_table(table, sums, counts[0], basis.shape[0], dots)


def closing_body(counts, table, coarse, scalars, mine, weights, out_table, out_scalars):
    modes = coarse.shape[0]
    totals = coarse_weights(weights, table, coarse, counts[2])
    e1, z1y1, z1q0, z0y1, r1s, y1s, q0s, r1m0, y1m0, q0m0 = (
        spread(totals, modes + i) for i in range(10)
    )
    e0, z0q0, step0 = scalars[0:1, :], scalars[1:2, :], scalars[2:3, :]
    beta = e1 / e0
    step = e1 / (z1y1 + beta * (z1q0 + z0y1) + beta * beta * z0q0)
    p_y1 = own_row(table, counts[1])
    p_q1 = p_y1 + beta * mine[1:2, :]
    side = jnp.broadcast_to(step * p_q1 - mine[0:1, :], (8, LANES))
    share = jnp.dot(
        side[:, :modes], weights[...], precision=precise, preferred_element_type=F32
    )
    out_table[...] = jnp.broadcast_to(share[0:1, :], out_table.shape)
    q1m1 = y1s + beta * (y1m0 + q0s) + beta * beta * q0m0
    known = step * q1m1 - (z1y1 + beta * z1q0) - (r1s + beta * r1m0)
    rows = [e1, beta, step, step0, known, jnp.zeros((3, LANES), F32)]
    out_scalars[...] = jnp.concatenate(rows, axis=0)


def finish_body(
    scalars,
    weights,
    basis,
    search0,
    image0,
    answer0,
    residual1,
    search1,
    image1,
    solved1,
    solution_out,
    residual_out,
    search_out,
    direction,
):
    beta, step, step0 = scalars[1:2, :], scalars[2:3, :], scalars[3:4, :]
    direction[...] = search1[...] + beta * search0[...]
    solution_out[...] = step0 * search0[...] + step * direction[...]
    residual_out[...] = residual1[...] - step * (image1[...] + beta * image0[...])
    answer1 = solved1[...] + expand(weights, basis)
    search_out[...] = search1[...] - step * (answer1 + beta * answer0[...])


def last_body(table, scalars, search, direction, out):
    e1, step, known = scalars[0:1, :], scalars[2:3, :], scalars[4:5, :]
    shares = jnp.sum(table[...], axis=0, keepdims=True)
    energy = e1 + step * (shares + known)
    out[...] = search[...] + energy / e1 * direction[...]


def local(
    right_side,
    stiffness,
    columns,
    margin_rows,
    local_inverse,
    margin_inverse,
    basis,
    coarse_counts,
    coarse_inverse,
):
    slabs, groups = lax.axis_size("slab"), lax.axis_size("grp")
    width = margin_rows.shape[2]
    size, rows = right_side.shape
    modes = basis.shape[0]
    half = groups // 2
    depth = size * width // LANES
    slab = lax.axis_index("slab")
    place = jnp.stack([lax.axis_index("grp"), slab]).astype(I32)
    counts = jnp.stack([coarse_counts[0], slab, coarse_counts[0]]).astype(I32)

    def pairs(low_step):
        found = []
        for s in range(slabs):
            for g in range(groups):
                other = s + (low_step if g < half else -low_step)
                if 0 <= other < slabs:
                    found.append((s * groups + g, other * groups + g))
        return found

    def exchange(table, axes):
        peers = table.shape[0]
        return lax.all_to_all(table.reshape(peers, 1, LANES), axes, 0, 0).reshape(peers, LANES)

    def gather(rim, send):
        rim = lax.ppermute(rim, AXES, pairs(-1))
        send = send.at[:, size:, :].set(jnp.broadcast_to(rim, (groups, depth, LANES)))
        return lax.all_to_all(send, "grp", 0, 0)

    field, table_of = ((size, rows), F32), ((slabs * groups, LANES), F32)
    small, rim_of = ((8, LANES), F32), ((depth, LANES), F32)
    send_of = ((groups, size + depth, LANES), F32)
    sums = pltpu.VMEM((LANES, LANES), F32)
    weights_of = pltpu.VMEM((modes, LANES), F32)
    picked = pltpu.VMEM((columns.shape[0], size, LANES), F32)

    table, packed, meta = call(
        begin_body,
        [table_of, ((size, depth, LANES), F32), ((8, LANES), I32)],
        [SMEM] * 3 + [VMEM] * 3,
        place,
        margin_rows,
        counts,
        right_side,
        basis,
        margin_inverse,
        scratch=[sums],
        groups=groups,
        rows=rows,
    )
    table = exchange(table, AXES)
    packed = lax.ppermute(packed, AXES, pairs(1))
    inverse, solved = call(
        inverse_body,
        [((size, size, rows), F32), field],
        [VMEM] * 4,
        meta,
        local_inverse,
        packed,
        right_side,
        width=width,
    )
    z0, mine, rim, send = call(
        first_body,
        [field, small, rim_of, send_of],
        [SMEM] * 2 + [VMEM] * 5,
        place,
        counts,
        table,
        coarse_inverse,
        basis,
        solved,
        meta,
        scratch=[weights_of],
        width=width,
    )

    def stiff(got, vectors, dots):
        return call(
            stiff_body,
            [field, field, table_of],
            [SMEM] + [VMEM] * (5 + len(vectors)),
            counts,
            got,
            columns,
            stiffness,
            basis,
            inverse,
            *vectors,
            scratch=[picked, sums],
            others=len(vectors),
            pairs=dots,
            width=width,
        )

    q0, solved, table = stiff(gather(rim, send), [z0, right_side], [(1, 0), (0, 2)])
    m0, r1, z1, mine, scalars, rim, send = call(
        second_body,
        [field, field, field, small, small, rim_of, send_of],
        [SMEM] * 2 + [VMEM] * 9,
        place,
        counts,
        exchange(table, AXES),
        coarse_inverse,
        basis,
        solved,
        meta,
        right_side,
        z0,
        q0,
        mine,
        scratch=[weights_of],
        width=width,
    )
    dots = [(1, 0), (0, 5), (0, 3), (2, 5), (1, 6), (5, 6), (3, 6), (1, 4), (5, 4), (3, 4)]
    y1, solved, table = stiff(gather(rim, send), [z1, r1, z0, q0, m0], dots)
    weights, table, scalars = call(
        closing_body,
        [((modes, LANES), F32), ((slabs, LANES), F32), small],
        [SMEM] + [VMEM] * 4,
        counts,
        exchange(table, AXES),
        coarse_inverse,
        scalars,
        mine,
    )
    x2, r2, z2, d1 = call(
        finish_body,
        [field] * 4,
        [VMEM] * 10,
        scalars,
        weights,
        basis,
        z0,
        q0,
        m0,
        r1,
        z1,
        y1,
        solved,
    )
    (d2,) = call(
        last_body, [field], [VMEM] * 4, exchange(table, "slab"), scalars, z2, d1
    )
    return x2, r2, d2


def solution(mesh):
    in_specs = (
        P(None, AXES),
        P(None, None, None, AXES),
        P(None, AXES),
        P("slab", None, None),
        P(None, None, AXES),
        P(None, None, "slab"),
        P(None, None, AXES),
        P("slab"),
        P("slab", None),
    )
    out_specs = (P(None, AXES),) * 3
    return jax.shard_map(local, mesh=mesh, in_specs=in_specs, out_specs=out_specs, check_vma=False)
```

time: 209 us -> 160 us (0.77)
  blocking collectives: 19.2 us -> 72.4 us
  waiting for transfers between devices: 60.7 us -> 17.2 us
  Pallas kernels: 0 us -> 37.6 us
  local copies, waits for them, and re-layouts: 29 us -> 3.35 us
  starting transfers between devices: 48.2 us -> 26.6 us
  other arithmetic: 21.8 us -> 1.25 us
  matrix products: 14.9 us -> 0 us
  between operations: 13.7 us -> 1.35 us
    all_to_all x1 -> x4, blocking collectives: 19.2 us -> 72.4 us  [the longest x2 38.9 us: exchange(): lax.all_to_all(table.reshape(peers, 1, LANES), axes, 0, 0)]
    pallas_call x0 -> x9, Pallas kernels: none -> 37.6 us  [call(): pl.pallas_call(functools.partial(body, **static), out_shape=shapes, in_sp...]
    all_to_all x5 -> x2, waiting for transfers between devices: 47 us -> 11.8 us  [exchange(): lax.all_to_all(table.reshape(peers, 1, LANES), axes, 0, 0)]
    all_to_all x5 -> x2, starting transfers between devices: 40.3 us -> 17.2 us  [exchange(): lax.all_to_all(table.reshape(peers, 1, LANES), axes, 0, 0)]
    dot_general x12 -> x0, matrix products: 14.9 us -> none  [ein(): jnp.einsum(pattern, *operands, precision=precise, preferred_element_type=...]
    dot_general x4 -> x0, other arithmetic: 10.7 us -> none  [ein(): jnp.einsum(pattern, *operands, precision=precise, preferred_element_type=...]
    ppermute x3, waiting for transfers between devices: 13.7 us -> 5.35 us  [the longest x2 5.34 us: gather(): rim = lax.ppermute(rim, AXES, pairs(-1))]
    concatenate x1 -> x0, local copies, waits for them, and re-layouts: 6.36 us -> none  [share(): row = jnp.concatenate([projected, jnp.stack(dots)]) if dots else projected]
  transfers between devices with their start and end apart: 8 -> 5, of which waited for: 8 -> 4; matrix products, arithmetic and copies ran while one was open for 5% -> 0% of each run, Pallas kernels for 0% -> 5%
where the time goes in v2:
time: 160 us
  blocking collectives  72.4 us (45%)
  Pallas kernels  37.6 us (24%)
  starting transfers between devices  26.6 us (17%)
  waiting for transfers between devices  17.2 us (11%)
  local copies, waits for them, and re-layouts  3.35 us (2%)
    all_to_all x2, blocking collectives, exchange(): lax.all_to_all(table.reshape(peers, 1, LANES), axes, 0, 0)  38.9 us
    pallas_call x9, Pallas kernels, call(): pl.pallas_call(functools.partial(body, **static), out_shape=shapes, in_sp...  37.6 us
    all_to_all x2, blocking collectives, gather(): return lax.all_to_all(send, 'grp', 0, 0)  33.5 us
    all_to_all x2, starting transfers between devices, exchange(): lax.all_to_all(table.reshape(peers, 1, LANES), axes, 0, 0)  17.2 us
    all_to_all x2, waiting for transfers between devices, exchange(): lax.all_to_all(table.reshape(peers, 1, LANES), axes, 0, 0)  11.8 us
    ppermute x2, waiting for transfers between devices, gather(): rim = lax.ppermute(rim, AXES, pairs(-1))  5.34 us
    ppermute x2, starting transfers between devices, gather(): rim = lax.ppermute(rim, AXES, pairs(-1))  4.98 us
    ppermute x1, starting transfers between devices, local(): packed = lax.ppermute(packed, AXES, pairs(1))  4.5 us
  transfers between devices with their start and end apart: 5, of which 4 were waited for; matrix products, arithmetic and copies ran while one was open for 0% of the time, Pallas kernels for 5%

profile of v2, /device:TPU:1, one launch (start us, length us, event | category | flops | bytes accessed | tf_op | source)
XLA Modules:
  0.0 159.7 jit_solution(6084526401246914316)
XLA Ops:
  1.3 0.7 pad_add_fusion.counts
  1.9 0.6 pad_add_fusion.1.place
  2.5 5.7 %shard_map.112 = (f32[256,128]{1,0:T(8,128)}, f32[64,16,128]{2,1,0:T(8,128)}, s32[8,128]{1,0:T(8,128)}) custom-call(s32[2]{0:T(128)} %pad_add_fusion.1.place, s32[1,2,32]{2,1,0:T(2,128)} %margin_rows.1, s32[3]{0:T(128)} %pad_add_fusion.counts, f32[64,128]{1,0:T(8,128)} %field.5, bf16[64,64,128]{2,1,0:T(8,128)(2,1)} %basis.11, bf16[64,64,64]{2,1,0:T(8,128)(2,1)} %margin.1), custom_call_target="tpu_custom_call" | custom-call | bytes 1605908 | tf_op jit(solution)/shard_map/pallas_call | solution.py:21
  8.2 4.5 %collective-permute-start = (f32[64,16,128]{2,1,0:T(8,128)}, f32[64,16,128]{2,1,0:T(8,128)S(1)}, u32[]{:S(2)}, u32[]{:S(2)}) collective-permute-start(f32[64,16,128]{2,1,0:T(8,128)} %get-tuple-element.58), channel_id=1, source_target_pairs={{0,8},{1,9},{2,10},{3,11},{8,16},{9,17},{10,18},{11,19},{12,4},{13... | collective-permute-start | bytes 1572872 | tf_op jit(solution)/shard_map/ppermute | solution.py:444
  12.7 13.2 %all-to-all-start = ((f32[256,1,128]{2,1,0:T(1,128)}), f32[256,1,128]{2,1,0:T(1,128)S(1)}, u32[]{:S(2)}, u32[]{:S(2)}) async-start(f32[256,1,128]{2,1,0:T(1,128)} %bitcast.21), calls=%async_computation | async-start | bytes 262144 | tf_op jit(solution)/shard_map/all_to_all | solution.py:415
  25.9 0.0 collective-permute-done.packed
  25.9 0.0 copy-start
  25.9 0.8 copy-done
  26.7 5.3 %shard_map.113 = (f32[64,64,128]{2,1,0:T(8,128)}, f32[64,128]{1,0:T(8,128)}) custom-call(s32[8,128]{1,0:T(8,128)} %get-tuple-element.57.meta, bf16[64,64,128]{2,1,0:T(8,128)(2,1)} %local_inverse.1, f32[64,16,128]{2,1,0:T(8,128)} %copy-done, f32[64,128]{1,0:T(8,128)} %field.5), custom_call_target="tpu_custom_call" | custom-call | bytes 1609728 | tf_op jit(solution)/shard_map/pallas_call | solution.py:21
  32.0 6.9 %all-to-all-done = f32[256,1,128]{2,1,0:T(1,128)S(1)} async-done(((f32[256,1,128]{2,1,0:T(1,128)}), f32[256,1,128]{2,1,0:T(1,128)S(1)}, u32[]{:S(2)}, u32[]{:S(2)}) %all-to-all-start) | async-done | bytes 131104 | tf_op jit(solution)/shard_map/all_to_all | solution.py:415
  38.9 0.0 copy-start.1
  38.9 0.6 copy-done.1
  39.6 2.8 %shard_map.114 = (f32[64,128]{1,0:T(8,128)}, f32[8,128]{1,0:T(8,128)}, f32[16,128]{1,0:T(8,128)}, f32[8,80,128]{2,1,0:T(8,128)}) custom-call(s32[2]{0:T(128)} %pad_add_fusion.1.place, s32[3]{0:T(128)} %pad_add_fusion.counts, f32[256,128]{1,0:T(8,128)} %bitcast.18, f32[64,2048]{1,0:T(8,128)} %coarse.5, bf16[64,64,128]{2,1,0:T(8,128)(2,1)} %basis.11, ...), custom_call_target="tpu_custom_call" | custom-call | bytes 1740820 | tf_op jit(solution)/shard_map/pallas_call | solution.py:21
  42.3 2.4 %collective-permute-start.1 = (f32[16,128]{1,0:T(8,128)}, f32[16,128]{1,0:T(8,128)S(1)}, u32[]{:S(2)}, u32[]{:S(2)}) collective-permute-start(f32[16,128]{1,0:T(8,128)} %get-tuple-element.61), channel_id=1, source_target_pairs={{4,12},{5,13},{6,14},{7,15},{8,0},{9,1},{10,2},{11,3},{12,20},{13,... | collective-permute-start | bytes 24584 | tf_op jit(solution)/shard_map/ppermute | solution.py:418
  44.8 2.7 %collective-permute-done.1 = f32[16,128]{1,0:T(8,128)S(1)} collective-permute-done((f32[16,128]{1,0:T(8,128)}, f32[16,128]{1,0:T(8,128)S(1)}, u32[]{:S(2)}, u32[]{:S(2)}) %collective-permute-start.1) | collective-permute-done | bytes 8224 | tf_op jit(solution)/shard_map/ppermute | solution.py:418
  47.5 0.6 broadcast_dynamic-update-slice_fusion.1
  48.2 16.7 %all_to_all.30.got = f32[8,80,128]{2,1,0:T(8,128)} all-to-all(f32[8,80,128]{2,1,0:T(8,128)} %broadcast_dynamic-update-slice_fusion.1), channel_id=1, replica_groups=mesh['slab'=32,'grp'=8] {'grp'}, dimensions={0} | all-to-all | bytes 655360 | tf_op jit(solution)/shard_map/all_to_all | solution.py:420
  64.8 7.6 %shard_map.115 = (f32[64,128]{1,0:T(8,128)}, f32[64,128]{1,0:T(8,128)}, f32[256,128]{1,0:T(8,128)}) custom-call(s32[3]{0:T(128)} %pad_add_fusion.counts, f32[8,80,128]{2,1,0:T(8,128)} %all_to_all.30.got, s32[7,128]{1,0:T(8,128)} %columns.3, bf16[7,64,64,128]{3,2,1,0:T(8,128)(2,1)} %stiffness.3, bf16[64,64,128]{2,1,0:T(8,128)(2,1)} %basis.11, ...), custom_call_target="tpu_custom_call" | custom-call | bytes 10882572 | tf_op jit(solution)/shard_map/pallas_call | solution.py:21
  72.5 20.0 %all_to_all.31 = f32[256,1,128]{2,1,0:T(1,128)} all-to-all(f32[256,1,128]{2,1,0:T(1,128)} %bitcast.23), channel_id=1, replica_groups=mesh['slab'=32,'grp'=8] {'slab','grp'}, dimensions={0} | all-to-all | bytes 262144 | tf_op jit(solution)/shard_map/all_to_all | solution.py:415
  92.4 2.8 %shard_map.116 = (f32[64,128]{1,0:T(8,128)}, f32[64,128]{1,0:T(8,128)}, f32[64,128]{1,0:T(8,128)}, f32[8,128]{1,0:T(8,128)}, f32[8,128]{1,0:T(8,128)}, /*index=5*/f32[16,128]{1,0:T(8,128)}, f32[8,80,128]{2,1,0:T(8,128)}) custom-call(s32[2]{0:T(128)} %pad_add_fusion.1.place, s32[3]{0:T(128)} %pad_add_fusion.counts, f32[256,128]{1,0:T(8,128)} %bitcast.19, ...), custom_call_target="tpu_custom_call" | custom-call | bytes 1843220 | tf_op jit(solution)/shard_map/pallas_call | solution.py:21
  95.3 2.5 %collective-permute-start.2 = (f32[16,128]{1,0:T(8,128)}, f32[16,128]{1,0:T(8,128)S(1)}, u32[]{:S(2)}, u32[]{:S(2)}) collective-permute-start(f32[16,128]{1,0:T(8,128)} %get-tuple-element.69), channel_id=1, source_target_pairs={{4,12},{5,13},{6,14},{7,15},{8,0},{9,1},{10,2},{11,3},{12,20},{13,... | collective-permute-start | bytes 24584 | tf_op jit(solution)/shard_map/ppermute | solution.py:418
  97.8 2.6 %collective-permute-done.2 = f32[16,128]{1,0:T(8,128)S(1)} collective-permute-done((f32[16,128]{1,0:T(8,128)}, f32[16,128]{1,0:T(8,128)S(1)}, u32[]{:S(2)}, u32[]{:S(2)}) %collective-permute-start.2) | collective-permute-done | bytes 8224 | tf_op jit(solution)/shard_map/ppermute | solution.py:418
  100.4 0.6 broadcast_dynamic-update-slice_fusion
  101.1 16.8 %all_to_all.32.got = f32[8,80,128]{2,1,0:T(8,128)} all-to-all(f32[8,80,128]{2,1,0:T(8,128)} %broadcast_dynamic-update-slice_fusion), channel_id=1, replica_groups=mesh['slab'=32,'grp'=8] {'grp'}, dimensions={0} | all-to-all | bytes 655360 | tf_op jit(solution)/shard_map/all_to_all | solution.py:420
  117.9 7.7 %shard_map.117 = (f32[64,128]{1,0:T(8,128)}, f32[64,128]{1,0:T(8,128)}, f32[256,128]{1,0:T(8,128)}) custom-call(s32[3]{0:T(128)} %pad_add_fusion.counts, f32[8,80,128]{2,1,0:T(8,128)} %all_to_all.32.got, s32[7,128]{1,0:T(8,128)} %columns.3, bf16[7,64,64,128]{3,2,1,0:T(8,128)(2,1)} %stiffness.3, bf16[64,64,128]{2,1,0:T(8,128)(2,1)} %basis.11, ...), custom_call_target="tpu_custom_call" | custom-call | bytes 10980876 | tf_op jit(solution)/shard_map/pallas_call | solution.py:21
  125.6 18.9 %all_to_all.33 = f32[256,1,128]{2,1,0:T(1,128)} all-to-all(f32[256,1,128]{2,1,0:T(1,128)} %bitcast.22), channel_id=1, replica_groups=mesh['slab'=32,'grp'=8] {'slab','grp'}, dimensions={0} | all-to-all | bytes 262144 | tf_op jit(solution)/shard_map/all_to_all | solution.py:415
  144.5 2.1 %shard_map.118 = (f32[64,128]{1,0:T(8,128)}, f32[32,128]{1,0:T(8,128)}, f32[8,128]{1,0:T(8,128)}) custom-call(s32[3]{0:T(128)} %pad_add_fusion.counts, f32[256,128]{1,0:T(8,128)} %bitcast.20, f32[64,2048]{1,0:T(8,128)} %coarse.5, f32[8,128]{1,0:T(8,128)} %get-tuple-element.74.scalars, f32[8,128]{1,0:T(8,128)} %get-tuple-element.75.mine), custom_call_target="tpu_custom_call" | custom-call | bytes 663564 | tf_op jit(solution)/shard_map/pallas_call | solution.py:21
  146.6 4.0 %all-to-all-start.5 = ((f32[32,1,128]{2,1,0:T(1,128)}), f32[32,1,128]{2,1,0:T(1,128)S(1)}, u32[]{:S(2)}, u32[]{:S(2)}) async-start(f32[32,1,128]{2,1,0:T(1,128)} %bitcast.25), calls=%async_computation.5 | async-start | bytes 32768 | tf_op jit(solution)/shard_map/all_to_all | solution.py:415
  150.6 2.2 %shard_map.119 = (f32[64,128]{1,0:T(8,128)}, f32[64,128]{1,0:T(8,128)}, f32[64,128]{1,0:T(8,128)}, f32[64,128]{1,0:T(8,128)}) custom-call(f32[8,128]{1,0:T(8,128)} %get-tuple-element.76.scalars, f32[64,128]{1,0:T(8,128)} %get-tuple-element.77.weights, bf16[64,64,128]{2,1,0:T(8,128)(2,1)} %basis.11, ...), custom_call_target="tpu_custom_call" | custom-call | bytes 1314816 | tf_op jit(solution)/shard_map/pallas_call | solution.py:21
  152.8 4.9 %all-to-all-done.5 = f32[32,1,128]{2,1,0:T(1,128)S(1)} async-done(((f32[32,1,128]{2,1,0:T(1,128)}), f32[32,1,128]{2,1,0:T(1,128)S(1)}, u32[]{:S(2)}, u32[]{:S(2)}) %all-to-all-start.5) | async-done | bytes 16416 | tf_op jit(solution)/shard_map/all_to_all | solution.py:415
  157.7 0.0 copy-start.2
  157.7 0.6 copy-done.2
  158.3 1.4 shard_map.120
Async XLA Ops:
  8.2 17.7 %collective-permute-start = (f32[64,16,128]{2,1,0:T(8,128)}, f32[64,16,128]{2,1,0:T(8,128)S(1)}, u32[]{:S(2)}, u32[]{:S(2)}) collective-permute-start(f32[64,16,128]{2,1,0:T(8,128)} %get-tuple-element.58), channel_id=1, source_target_pairs={{0,8},{1,9},{2,10},{3,11},{8,16},{9,17},{10,18},{11,19},{12,4},{13... | collective-permute-start | bytes 1572872 | tf_op jit(solution)/shard_map/ppermute | solution.py:444
  12.7 26.2 %all-to-all-start = ((f32[256,1,128]{2,1,0:T(1,128)}), f32[256,1,128]{2,1,0:T(1,128)S(1)}, u32[]{:S(2)}, u32[]{:S(2)}) async-start(f32[256,1,128]{2,1,0:T(1,128)} %bitcast.21), calls=%async_computation | async-start | bytes 262144 | tf_op jit(solution)/shard_map/all_to_all | solution.py:415
  25.9 0.8 copy-start
  38.9 0.6 copy-start.1
  42.3 5.2 %collective-permute-start.1 = (f32[16,128]{1,0:T(8,128)}, f32[16,128]{1,0:T(8,128)S(1)}, u32[]{:S(2)}, u32[]{:S(2)}) collective-permute-start(f32[16,128]{1,0:T(8,128)} %get-tuple-element.61), channel_id=1, source_target_pairs={{4,12},{5,13},{6,14},{7,15},{8,0},{9,1},{10,2},{11,3},{12,20},{13,... | collective-permute-start | bytes 24584 | tf_op jit(solution)/shard_map/ppermute | solution.py:418
  95.3 5.2 %collective-permute-start.2 = (f32[16,128]{1,0:T(8,128)}, f32[16,128]{1,0:T(8,128)S(1)}, u32[]{:S(2)}, u32[]{:S(2)}) collective-permute-start(f32[16,128]{1,0:T(8,128)} %get-tuple-element.69), channel_id=1, source_target_pairs={{4,12},{5,13},{6,14},{7,15},{8,0},{9,1},{10,2},{11,3},{12,20},{13,... | collective-permute-start | bytes 24584 | tf_op jit(solution)/shard_map/ppermute | solution.py:418
  146.6 11.0 %all-to-all-start.5 = ((f32[32,1,128]{2,1,0:T(1,128)}), f32[32,1,128]{2,1,0:T(1,128)S(1)}, u32[]{:S(2)}, u32[]{:S(2)}) async-start(f32[32,1,128]{2,1,0:T(1,128)} %bitcast.25), calls=%async_computation.5 | async-start | bytes 32768 | tf_op jit(solution)/shard_map/all_to_all | solution.py:415
  157.7 0.6 copy-start.2

commit v3 on v2

--- a/solution.py
+++ b/solution.py
@@ -5,17 +5,21 @@
 from jax import lax
 from jax.experimental import pallas as pl
 from jax.experimental.pallas import tpu as pltpu
-from jax.sharding import PartitionSpec as P
-
-AXES = ("slab", "grp")
+from jax.sharding import Mesh, PartitionSpec as P
+
+SLAB = ("plane", "core")
+AXES = SLAB + ("grp",)
 F32, I32 = jnp.float32, jnp.int32
 LANES = 128
+MIB = 1 << 20
+FLOPS = 4 * 10**9
 VMEM = pl.BlockSpec(memory_space=pltpu.VMEM)
 SMEM = pl.BlockSpec(memory_space=pltpu.SMEM)
+HBM = pl.BlockSpec(memory_space=pltpu.HBM)
 precise = lax.Precision.HIGHEST
 
 
-def call(body, outs, specs, *operands, scratch=(), flops=0, **static):
+def call(body, outs, specs, *operands, scratch=(), vmem=16, **static):
     shapes = [jax.ShapeDtypeStruct(shape, dtype) for shape, dtype in outs]
     read = sum(x.size * x.dtype.itemsize for x in operands)
     return pl.pallas_call(
@@ -24,12 +28,28 @@
         in_specs=specs,
         out_specs=[VMEM] * len(shapes),
         scratch_shapes=list(scratch),
-        cost_estimate=pl.CostEstimate(flops=flops, bytes_accessed=read, transcendentals=0),
+        compiler_params=pltpu.CompilerParams(vmem_limit_bytes=vmem * MIB),
+        cost_estimate=pl.CostEstimate(flops=FLOPS, bytes_accessed=read, transcendentals=0),
     )(*operands)
 
 
 def tile_sum(parts):
-    return jnp.concatenate([jnp.sum(part, axis=0, keepdims=True) for part in parts], axis=0)
+    row = lax.broadcasted_iota(I32, (8, LANES), 0)
+    sums = []
+    for low, high in zip(parts[:4], parts[4:]):
+        kept, moved = jnp.where(row < 4, low, high), jnp.where(row < 4, high, low)
+        sums.append(kept + pltpu.roll(moved, 4, 0))
+    for shift in (2, 1):
+        half = len(sums) // 2
+        sums = [
+            jnp.where(
+                row & shift == 0,
+                low + pltpu.roll(low, 8 - shift, 0),
+                high + pltpu.roll(high, shift, 0),
+            )
+            for low, high in zip(sums[:half], sums[half:])
+        ]
+    return sums[0]
 
 
 def lane_index(rows=8):
@@ -55,7 +75,7 @@
             acc = jnp.zeros((16, LANES), F32)
             for t in range(0, size, 16):
                 acc += basis_ref[first + r, t : t + 16, :].astype(F32) * vector[t : t + 16]
-            parts.append(acc)
+            parts.append(acc[:8] + acc[8:])
         sums_ref[pl.ds(first, 8), :] = tile_sum(parts)
         return carry
 
@@ -97,15 +117,31 @@
 
 
 def begin_body(
-    place, margin_rows, counts, field, basis, margin, table, packed, meta, sums, *, groups, rows
+    margin_rows,
+    counts,
+    field_hbm,
+    basis_hbm,
+    margin_hbm,
+    table,
+    packed,
+    meta,
+    sums,
+    field,
+    basis,
+    margin,
+    sems,
+    *,
+    groups,
+    rows,
 ):
+    pairs = [(field_hbm, field), (basis_hbm, basis), (margin_hbm, margin)]
+    copies = [pltpu.make_async_copy(a, b, sems.at[i]) for i, (a, b) in enumerate(pairs)]
+    for copy in copies:
+        copy.start()
     size = field.shape[0]
     width = margin_rows.shape[2]
-    group = place[0]
+    group = lax.axis_index("grp")
     face = jnp.where(group < groups // 2, 0, 1)
-    project_into(sums, basis, field[...])
-    write_table(table, sums, counts[0], basis.shape[0], [])
-
     lane = lane_index(1)
     slot, owned = jnp.zeros((1, LANES), I32), jnp.zeros((1, LANES), I32)
     source = jnp.full((1, LANES), -1, I32)
@@ -119,51 +155,47 @@
     source = jnp.clip(source, 0, rows - 1)
     meta[...] = jnp.concatenate([slot, owned, source, inside, jnp.zeros((4, LANES), I32)], axis=0)
 
+    copies[0].wait()
+    copies[1].wait()
+    project_into(sums, basis, field[...])
+    write_table(table, sums, counts[0], basis.shape[0], [])
+    copies[2].wait()
     parts = LANES // width
     depth = size // parts
-    lanes = lane_index(depth)
-    full = LANES // margin.shape[2]
-
-    def one(i, carry):
-        result = jnp.zeros((depth, LANES), F32)
-        for a in range(parts):
-            block = margin[i, a * depth : (a + 1) * depth, :].astype(F32)
-            block = jnp.concatenate([block] * full, axis=1)
-            upper = pltpu.roll(block, (a * width - width) % LANES, 1)
-            lower = pltpu.roll(block, a * width, 1)
-            part = jnp.where(face == 0, upper, lower)
-            result = jnp.where((lanes >= a * width) & (lanes < (a + 1) * width), part, result)
-        packed[i] = result
-        return carry
-
-    lax.fori_loop(0, size, one, 0, unroll=4)
+    given = lax.broadcasted_iota(I32, (margin.shape[2], LANES), 0)
+    lanes = lane_index(margin.shape[2])
+    place = given == lanes % width + jnp.where(face == 0, width, 0)
+    result = jnp.zeros((size * depth, LANES), F32)
+    for a in range(parts):
+        block = margin[:, a * depth : (a + 1) * depth, :].reshape(size * depth, margin.shape[2])
+        chosen = (place & (lanes // width == a)).astype(F32).astype(jnp.bfloat16)
+        result += jnp.dot(block, chosen, preferred_element_type=F32)
+    packed[...] = result.reshape(size, depth, LANES)
 
 
 def inverse_body(meta, local_inverse, packed, field, inverse, solved, *, width):
     size, depth, _ = packed.shape
-    slot = meta[0:1, :]
-    owned = jnp.broadcast_to(meta[1:2, :], (depth, LANES)) > 0
-
-    def one(i, carry):
-        block = packed[i]
-        for a in range(size // depth):
-            extra = jnp.where(owned, pick_lanes(block, slot + a * width), 0.0)
-            own = local_inverse[i, a * depth : (a + 1) * depth, :].astype(F32)
-            inverse[i, a * depth : (a + 1) * depth, :] = own + extra
-        return carry
-
-    lax.fori_loop(0, size, one, 0, unroll=4)
+    row = lax.broadcasted_iota(I32, (LANES, LANES), 0)
+    place = (row % width == meta[0:1, :]) & (meta[1:2, :] > 0)
+    blocks = packed[...].reshape(size * depth, LANES).astype(jnp.bfloat16)
+    for a in range(size // depth):
+        chosen = (place & (row // width == a)).astype(F32).astype(jnp.bfloat16)
+        extra = jnp.dot(blocks, chosen, preferred_element_type=F32)
+        own = local_inverse[:, a * depth : (a + 1) * depth, :].astype(F32)
+        inverse[:, a * depth : (a + 1) * depth, :] = own + extra.reshape(size, depth, LANES)
     block_product(solved, inverse, field[...])
 
 
-def coarse_weights(weights_ref, table, coarse, count):
+def coarse_weights(weights_ref, mine, other, coarse, count):
     modes = coarse.shape[0]
     lane = lane_index()
     accs = [jnp.zeros((8, LANES), F32) for _ in range(modes // 8)]
     totals = jnp.zeros((8, LANES), F32)
-    for m in range(table.shape[0] // 16):
-        even, odd = table[16 * m : 16 * m + 8, :], table[16 * m + 8 : 16 * m + 16, :]
-        totals += even + odd
+    first = lax.axis_index("core") == 0
+    for m in range(mine.shape[0] // 8):
+        own, twin = mine[8 * m : 8 * m + 8, :], other[8 * m : 8 * m + 8, :]
+        totals += own + twin
+        even, odd = jnp.where(first, own, twin), jnp.where(first, twin, own)
         both = jnp.where(lane < modes, even, pltpu.roll(odd, modes, 1))
         both = jnp.sum(both, axis=0, keepdims=True)
         for r in range(modes // 8):
@@ -196,8 +228,9 @@
     return jnp.concatenate(lax.fori_loop(0, modes // 8, eight, accs), axis=0)
 
 
-def own_row(table, slab):
-    return jnp.sum(table[pl.ds(pl.multiple_of(slab * 8, 8), 8), :], axis=0, keepdims=True)
+def own_row(table):
+    start = pl.multiple_of(lax.axis_index("plane") * 8, 8)
+    return jnp.sum(table[pl.ds(start, 8), :], axis=0, keepdims=True)
 
 
 def spread(row, lane):
@@ -221,18 +254,18 @@
 
 
 def first_body(
-    place, counts, table, coarse, basis, solved, meta, search, mine, rim, send, weights, *, width
+    counts, table, other, coarse, basis, solved, meta, search, mine, rim, send, weights, *, width
 ):
-    coarse_weights(weights, table, coarse, counts[0])
-    mine[...] = jnp.broadcast_to(own_row(table, place[1]), (8, LANES))
+    coarse_weights(weights, table, other, coarse, counts[0])
+    mine[...] = jnp.broadcast_to(own_row(table), (8, LANES))
     search[...] = solved[...] + expand(weights, basis)
     send_out(search[...], meta, rim, send, width=width)
 
 
 def second_body(
-    place,
     counts,
     table,
+    other,
     coarse,
     basis,
     solved,
@@ -253,10 +286,10 @@
     width,
 ):
     modes = basis.shape[0]
-    totals = coarse_weights(weights, table, coarse, counts[0])
+    totals = coarse_weights(weights, table, other, coarse, counts[0])
     energy, curve = spread(totals, modes), spread(totals, modes + 1)
     step = energy / curve
-    p_q0 = own_row(table, place[1])
+    p_q0 = own_row(table)
     p_r1 = mine0[0:1, :] - step * p_q0
     mine[...] = jnp.concatenate([p_r1, p_q0, jnp.zeros((6, LANES), F32)], axis=0)
     scalars[...] = jnp.concatenate([energy, curve, step, jnp.zeros((5, LANES), F32)], axis=0)
@@ -309,7 +342,7 @@
                 value = picked[k, t : t + 16, :]
                 for r in range(8):
                     accs[r] += stiffness[k, first + r, t : t + 16, :].astype(F32) * value
-        out_ref[pl.ds(first, 8), :] = tile_sum(accs)
+        out_ref[pl.ds(first, 8), :] = tile_sum([acc[:8] + acc[8:] for acc in accs])
         return carry
 
     lax.fori_loop(0, size // 8, eight, 0)
@@ -327,16 +360,16 @@
     write_table(table, sums, counts[0], basis.shape[0], dots)
 
 
-def closing_body(counts, table, coarse, scalars, mine, weights, out_table, out_scalars):
+def closing_body(counts, table, other, coarse, scalars, mine, weights, out_table, out_scalars):
     modes = coarse.shape[0]
-    totals = coarse_weights(weights, table, coarse, counts[2])
+    totals = coarse_weights(weights, table, other, coarse, counts[0])
     e1, z1y1, z1q0, z0y1, r1s, y1s, q0s, r1m0, y1m0, q0m0 = (
         spread(totals, modes + i) for i in range(10)
     )
     e0, z0q0, step0 = scalars[0:1, :], scalars[1:2, :], scalars[2:3, :]
     beta = e1 / e0
     step = e1 / (z1y1 + beta * (z1q0 + z0y1) + beta * beta * z0q0)
-    p_y1 = own_row(table, counts[1])
+    p_y1 = own_row(table)
     p_q1 = p_y1 + beta * mine[1:2, :]
     side = jnp.broadcast_to(step * p_q1 - mine[0:1, :], (8, LANES))
     share = jnp.dot(
@@ -391,15 +424,14 @@
     coarse_counts,
     coarse_inverse,
 ):
-    slabs, groups = lax.axis_size("slab"), lax.axis_size("grp")
+    planes, groups = lax.axis_size("plane"), lax.axis_size("grp")
+    slabs = planes * lax.axis_size("core")
     width = margin_rows.shape[2]
     size, rows = right_side.shape
     modes = basis.shape[0]
     half = groups // 2
     depth = size * width // LANES
-    slab = lax.axis_index("slab")
-    place = jnp.stack([lax.axis_index("grp"), slab]).astype(I32)
-    counts = jnp.stack([coarse_counts[0], slab, coarse_counts[0]]).astype(I32)
+    counts = coarse_counts
 
     def pairs(low_step):
         found = []
@@ -414,12 +446,16 @@
         peers = table.shape[0]
         return lax.all_to_all(table.reshape(peers, 1, LANES), axes, 0, 0).reshape(peers, LANES)
 
+    def share(table):
+        table = exchange(table, ("plane", "grp"))
+        return table, lax.ppermute(table, "core", ((0, 1), (1, 0)))
+
     def gather(rim, send):
         rim = lax.ppermute(rim, AXES, pairs(-1))
         send = send.at[:, size:, :].set(jnp.broadcast_to(rim, (groups, depth, LANES)))
         return lax.all_to_all(send, "grp", 0, 0)
 
-    field, table_of = ((size, rows), F32), ((slabs * groups, LANES), F32)
+    field, table_of = ((size, rows), F32), ((planes * groups, LANES), F32)
     small, rim_of = ((8, LANES), F32), ((depth, LANES), F32)
     send_of = ((groups, size + depth, LANES), F32)
     sums = pltpu.VMEM((LANES, LANES), F32)
@@ -429,18 +465,20 @@
     table, packed, meta = call(
         begin_body,
         [table_of, ((size, depth, LANES), F32), ((8, LANES), I32)],
-        [SMEM] * 3 + [VMEM] * 3,
-        place,
+        [SMEM] * 2 + [HBM] * 3,
         margin_rows,
         counts,
         right_side,
         basis,
         margin_inverse,
-        scratch=[sums],
+        scratch=[sums]
+        + [pltpu.VMEM(x.shape, x.dtype) for x in (right_side, basis, margin_inverse)]
+        + [pltpu.SemaphoreType.DMA((3,))],
+        vmem=62,
         groups=groups,
         rows=rows,
     )
-    table = exchange(table, AXES)
+    table, other = share(table)
     packed = lax.ppermute(packed, AXES, pairs(1))
     inverse, solved = call(
         inverse_body,
@@ -455,10 +493,10 @@
     z0, mine, rim, send = call(
         first_body,
         [field, small, rim_of, send_of],
-        [SMEM] * 2 + [VMEM] * 5,
-        place,
+        [SMEM] + [VMEM] * 6,
         counts,
         table,
+        other,
         coarse_inverse,
         basis,
         solved,
@@ -489,10 +527,9 @@
     m0, r1, z1, mine, scalars, rim, send = call(
         second_body,
         [field, field, field, small, small, rim_of, send_of],
-        [SMEM] * 2 + [VMEM] * 9,
-        place,
+        [SMEM] + [VMEM] * 10,
         counts,
-        exchange(table, AXES),
+        *share(table),
         coarse_inverse,
         basis,
         solved,
@@ -509,9 +546,9 @@
     weights, table, scalars = call(
         closing_body,
         [((modes, LANES), F32), ((slabs, LANES), F32), small],
-        [SMEM] + [VMEM] * 4,
+        [SMEM] + [VMEM] * 5,
         counts,
-        exchange(table, AXES),
+        *share(table),
         coarse_inverse,
         scalars,
         mine,
@@ -532,22 +569,24 @@
         solved,
     )
     (d2,) = call(
-        last_body, [field], [VMEM] * 4, exchange(table, "slab"), scalars, z2, d1
+        last_body, [field], [VMEM] * 4, exchange(table, SLAB), scalars, z2, d1
     )
     return x2, r2, d2
 
 
 def solution(mesh):
+    slabs, groups = mesh.devices.shape
+    mesh = Mesh(mesh.devices.reshape(slabs // 2, 2, groups), AXES)
     in_specs = (
         P(None, AXES),
         P(None, None, None, AXES),
         P(None, AXES),
-        P("slab", None, None),
+        P(SLAB, None, None),
         P(None, None, AXES),
-        P(None, None, "slab"),
+        P(None, None, SLAB),
         P(None, None, AXES),
-        P("slab"),
-        P("slab", None),
+        P(SLAB),
+        P(SLAB, None),
     )
     out_specs = (P(None, AXES),) * 3
     return jax.shard_map(local, mesh=mesh, in_specs=in_specs, out_specs=out_specs, check_vma=False)

time: 160 us -> 137 us (0.86)
  Pallas kernels: 37.6 us -> 14.1 us
  blocking collectives: 72.4 us -> 88.2 us
  starting transfers between devices: 26.6 us -> 17.6 us
  waiting for transfers between devices: 17.2 us -> 13.7 us
  local copies, waits for them, and re-layouts: 3.35 us -> 1.4 us
    pallas_call x9, Pallas kernels: 37.6 us -> 14.1 us  [call(): pl.pallas_call(functools.partial(body, **static), out_shape=shapes, in_sp...]
    all_to_all x2 -> x3, blocking collectives: 38.9 us -> 58.9 us  [exchange(): lax.all_to_all(table.reshape(peers, 1, LANES), axes, 0, 0)]
    all_to_all x2 -> x1, starting transfers between devices: 17.2 us -> 3.83 us  [exchange(): lax.all_to_all(table.reshape(peers, 1, LANES), axes, 0, 0)]
    all_to_all x2 -> x1, waiting for transfers between devices: 11.8 us -> 6.13 us  [exchange(): lax.all_to_all(table.reshape(peers, 1, LANES), axes, 0, 0)]
    ppermute x0 -> x3, starting transfers between devices: none -> 4.98 us  [share(): return (table, lax.ppermute(table, 'core', ((0, 1), (1, 0))))]
    all_to_all x2, blocking collectives: 33.5 us -> 29.3 us  [gather(): return lax.all_to_all(send, 'grp', 0, 0)]
    ppermute x0 -> x3, waiting for transfers between devices: none -> 1.81 us  [share(): return (table, lax.ppermute(table, 'core', ((0, 1), (1, 0))))]
  transfers between devices with their start and end apart: 5 -> 7, of which waited for: 4 -> 5; matrix products, arithmetic and copies ran while one was open for 0% -> 0% of each run, Pallas kernels for 5% -> 1%
where the time goes in v3:
time: 137 us; the launch traced here: 136 us
  blocking collectives  88.2 us (64%)
  starting transfers between devices  17.6 us (13%)
  Pallas kernels  14.1 us (10%)
  waiting for transfers between devices  13.7 us (10%)
  local copies, waits for them, and re-layouts  1.4 us (1%)
  between operations  1.39 us (1%)
    all_to_all x3, blocking collectives, exchange(): lax.all_to_all(table.reshape(peers, 1, LANES), axes, 0, 0)  58.9 us
    all_to_all x2, blocking collectives, gather(): return lax.all_to_all(send, 'grp', 0, 0)  29.3 us
    pallas_call x9, Pallas kernels, call(): pl.pallas_call(functools.partial(body, **static), out_shape=shapes, in_sp...  14.1 us
    all_to_all x1, waiting for transfers between devices, exchange(): lax.all_to_all(table.reshape(peers, 1, LANES), axes, 0, 0)  6.13 us
    ppermute x2, waiting for transfers between devices, gather(): rim = lax.ppermute(rim, AXES, pairs(-1))  5.74 us
    ppermute x3, starting transfers between devices, share(): return (table, lax.ppermute(table, 'core', ((0, 1), (1, 0))))  4.98 us
    ppermute x1, starting transfers between devices, local(): packed = lax.ppermute(packed, AXES, pairs(1))  4.51 us
    ppermute x2, starting transfers between devices, gather(): rim = lax.ppermute(rim, AXES, pairs(-1))  4.31 us
  transfers between devices with their start and end apart: 7, of which 5 were waited for; matrix products, arithmetic and copies ran while one was open for 0% of the time, Pallas kernels for 1%

profile of v3, /device:TPU:1, one launch (start us, length us, event | category | flops | bytes accessed | tf_op | source)
XLA Modules:
  0.0 136.4 jit_solution(963202454846399725)
XLA Ops:
  1.3 0.0 copy-start
  1.3 0.0 copy-start.3
  1.3 4.0 %shard_map.112 = (f32[128,128]{1,0:T(8,128)}, f32[64,16,128]{2,1,0:T(8,128)}, s32[8,128]{1,0:T(8,128)}) custom-call(s32[1,2,32]{2,1,0:T(2,128)} %margin_rows.1, s32[1]{0:T(128)S(6)} %copy.18.counts, f32[64,128]{1,0:T(8,128)} %field.3, bf16[64,64,128]{2,1,0:T(8,128)(2,1)} %basis.9, bf16[64,64,64]{2,1,0:T(8,128)(2,1)} %margin_hbm.1), custom_call_target="tpu_custom_call" | custom-call | flops 4000000000 | bytes 1605892 | tf_op jit(solution)/shard_map/pallas_call | solution.py:25
  5.3 4.5 %collective-permute-start.1 = (f32[64,16,128]{2,1,0:T(8,128)}, f32[64,16,128]{2,1,0:T(8,128)S(1)}, u32[]{:S(2)}, u32[]{:S(2)}) collective-permute-start(f32[64,16,128]{2,1,0:T(8,128)} %get-tuple-element.58), channel_id=1, source_target_pairs={{0,8},{1,9},{2,10},{3,11},{8,16},{9,17},{10,18},{11,19},{12,4},{13... | collective-permute-start | bytes 1572872 | tf_op jit(solution)/shard_map/ppermute | solution.py:482
  9.8 25.0 %all_to_all.30 = f32[128,1,128]{2,1,0:T(1,128)S(1)} all-to-all(f32[128,1,128]{2,1,0:T(1,128)} %bitcast.27), channel_id=1, replica_groups=mesh['plane'=16,'core'=2,'grp'=8] {'plane','grp'}, dimensions={0} | all-to-all | bytes 131072 | tf_op jit(solution)/shard_map/all_to_all | solution.py:447
  34.9 1.4 %collective-permute-start = (f32[128,128]{1,0:T(8,128)S(1)}, f32[128,128]{1,0:T(8,128)S(1)}, u32[]{:S(2)}, u32[]{:S(2)}) collective-permute-start(f32[128,128]{1,0:T(8,128)S(1)} %bitcast.16), channel_id=1, source_target_pairs={{0,8},{8,0},{1,9},{9,1},{2,10},{10,2},{3,11},{11,3},{4,12},{12,4},... | collective-permute-start | bytes 196616 | tf_op jit(solution)/shard_map/ppermute | solution.py:451
  36.3 0.0 collective-permute-done.1.packed
  36.3 0.0 copy-done
  36.3 0.0 copy-done.3
  36.3 0.0 copy-start.5
  36.3 0.7 copy-done.5
  37.0 0.0 copy-start.1
  37.0 0.0 copy-start.2
  37.0 0.0 slice-start
  37.0 0.7 shard_map.113
  37.6 0.0 collective-permute-done.other
  37.7 0.5 copy-done.1
  38.2 0.1 copy-done.2
  38.3 0.0 slice-start.1
  38.3 0.0 copy-start.4
  38.3 0.6 shard_map.114
  38.9 2.1 %collective-permute-start.2 = (f32[16,128]{1,0:T(8,128)S(1)}, f32[16,128]{1,0:T(8,128)S(1)}, u32[]{:S(2)}, u32[]{:S(2)}) collective-permute-start(f32[16,128]{1,0:T(8,128)S(1)} %get-tuple-element.61), channel_id=1, source_target_pairs={{4,12},{5,13},{6,14},{7,15},{8,0},{9,1},{10,2},{11,3},{12,20},{13,... | collective-permute-start | bytes 24584 | tf_op jit(solution)/shard_map/ppermute | solution.py:454
  41.0 3.0 %collective-permute-done.2 = f32[16,128]{1,0:T(8,128)S(1)} collective-permute-done((f32[16,128]{1,0:T(8,128)S(1)}, f32[16,128]{1,0:T(8,128)S(1)}, u32[]{:S(2)}, u32[]{:S(2)}) %collective-permute-start.2) | collective-permute-done | bytes 8224 | tf_op jit(solution)/shard_map/ppermute | solution.py:454
  44.0 14.5 %all_to_all.31.got = f32[8,80,128]{2,1,0:T(8,128)S(1)} all-to-all(f32[8,80,128]{2,1,0:T(8,128)S(1)} %broadcast_dynamic-update-slice_fusion.1), channel_id=1, replica_groups=mesh['plane'=16,'core'=2,'grp'=8] {'grp'}, dimensions={0} | all-to-all | bytes 655360 | tf_op jit(solution)/shard_map/all_to_all | solution.py:456
  58.5 0.0 slice-done
  58.5 0.0 slice-done.1
  58.5 0.0 copy-done.4
  58.5 2.8 %shard_map.115 = (f32[64,128]{1,0:T(8,128)S(1)}, f32[64,128]{1,0:T(8,128)S(1)}, f32[128,128]{1,0:T(8,128)S(1)}) custom-call(s32[1]{0:T(128)S(6)} %copy.18.counts, f32[8,80,128]{2,1,0:T(8,128)S(1)} %all_to_all.31.got, s32[7,128]{1,0:T(8,128)S(1)} %copy-done.4, bf16[7,64,64,128]{3,2,1,0:T(8,128)(2,1)S(1)} %bitcast.26, bf16[64,64,128]{2,1,0:T(8,128)(2,1)S(1)} %copy-done.1, ...), custom_call_target="tpu_custom_call" | custom-call | flops 4000000000 | bytes 10882564 | tf_op jit(solution)/shard_map/pallas_call | solution.py:25
  61.3 17.0 %all_to_all.32 = f32[128,1,128]{2,1,0:T(1,128)S(1)} all-to-all(f32[128,1,128]{2,1,0:T(1,128)S(1)} %bitcast.23), channel_id=1, replica_groups=mesh['plane'=16,'core'=2,'grp'=8] {'plane','grp'}, dimensions={0} | all-to-all | bytes 131072 | tf_op jit(solution)/shard_map/all_to_all | solution.py:447
  78.4 1.9 %collective-permute-start.3 = (f32[128,128]{1,0:T(8,128)S(1)}, f32[128,128]{1,0:T(8,128)S(1)}, u32[]{:S(2)}, u32[]{:S(2)}) collective-permute-start(f32[128,128]{1,0:T(8,128)S(1)} %bitcast.18), channel_id=1, source_target_pairs={{0,8},{8,0},{1,9},{9,1},{2,10},{10,2},{3,11},{11,3},{4,12},{12,4},... | collective-permute-start | bytes 196616 | tf_op jit(solution)/shard_map/ppermute | solution.py:451
  80.3 0.9 collective-permute-done.3.other
  81.2 0.6 shard_map.116
  81.8 2.3 %collective-permute-start.4 = (f32[16,128]{1,0:T(8,128)S(1)}, f32[16,128]{1,0:T(8,128)S(1)}, u32[]{:S(2)}, u32[]{:S(2)}) collective-permute-start(f32[16,128]{1,0:T(8,128)S(1)} %get-tuple-element.69), channel_id=1, source_target_pairs={{4,12},{5,13},{6,14},{7,15},{8,0},{9,1},{10,2},{11,3},{12,20},{13,... | collective-permute-start | bytes 24584 | tf_op jit(solution)/shard_map/ppermute | solution.py:454
  84.1 2.7 %collective-permute-done.4 = f32[16,128]{1,0:T(8,128)S(1)} collective-permute-done((f32[16,128]{1,0:T(8,128)S(1)}, f32[16,128]{1,0:T(8,128)S(1)}, u32[]{:S(2)}, u32[]{:S(2)}) %collective-permute-start.4) | collective-permute-done | bytes 8224 | tf_op jit(solution)/shard_map/ppermute | solution.py:454
  86.8 14.8 %all_to_all.33.got = f32[8,80,128]{2,1,0:T(8,128)S(1)} all-to-all(f32[8,80,128]{2,1,0:T(8,128)S(1)} %broadcast_dynamic-update-slice_fusion), channel_id=1, replica_groups=mesh['plane'=16,'core'=2,'grp'=8] {'grp'}, dimensions={0} | all-to-all | bytes 655360 | tf_op jit(solution)/shard_map/all_to_all | solution.py:456
  101.6 2.8 %shard_map.117 = (f32[64,128]{1,0:T(8,128)S(1)}, f32[64,128]{1,0:T(8,128)S(1)}, f32[128,128]{1,0:T(8,128)S(1)}) custom-call(s32[1]{0:T(128)S(6)} %copy.18.counts, f32[8,80,128]{2,1,0:T(8,128)S(1)} %all_to_all.33.got, s32[7,128]{1,0:T(8,128)S(1)} %copy-done.4, bf16[7,64,64,128]{3,2,1,0:T(8,128)(2,1)S(1)} %bitcast.26, bf16[64,64,128]{2,1,0:T(8,128)(2,1)S(1)} %copy-done.1, ...), custom_call_target="tpu_custom_call" | custom-call | flops 4000000000 | bytes 10980868 | tf_op jit(solution)/shard_map/pallas_call | solution.py:25
  104.4 16.9 %all_to_all.34 = f32[128,1,128]{2,1,0:T(1,128)S(1)} all-to-all(f32[128,1,128]{2,1,0:T(1,128)S(1)} %bitcast.22), channel_id=1, replica_groups=mesh['plane'=16,'core'=2,'grp'=8] {'plane','grp'}, dimensions={0} | all-to-all | bytes 131072 | tf_op jit(solution)/shard_map/all_to_all | solution.py:447
  121.3 1.7 %collective-permute-start.5 = (f32[128,128]{1,0:T(8,128)S(1)}, f32[128,128]{1,0:T(8,128)S(1)}, u32[]{:S(2)}, u32[]{:S(2)}) collective-permute-start(f32[128,128]{1,0:T(8,128)S(1)} %bitcast.20), channel_id=1, source_target_pairs={{0,8},{8,0},{1,9},{9,1},{2,10},{10,2},{3,11},{11,3},{4,12},{12,4},... | collective-permute-start | bytes 196616 | tf_op jit(solution)/shard_map/ppermute | solution.py:451
  122.9 0.9 collective-permute-done.5.other
  123.8 1.1 shard_map.118
  124.9 3.8 %all-to-all-start.5 = ((f32[32,1,128]{2,1,0:T(1,128)}), f32[32,1,128]{2,1,0:T(1,128)S(1)}, u32[]{:S(2)}, u32[]{:S(2)}) async-start(f32[32,1,128]{2,1,0:T(1,128)} %bitcast.10), calls=%async_computation.5 | async-start | bytes 32768 | tf_op jit(solution)/shard_map/all_to_all | solution.py:447
  128.7 0.8 shard_map.119
  129.6 6.1 %all-to-all-done.5 = f32[32,1,128]{2,1,0:T(1,128)S(1)} async-done(((f32[32,1,128]{2,1,0:T(1,128)}), f32[32,1,128]{2,1,0:T(1,128)S(1)}, u32[]{:S(2)}, u32[]{:S(2)}) %all-to-all-start.5) | async-done | bytes 16416 | tf_op jit(solution)/shard_map/all_to_all | solution.py:447
  135.7 0.6 shard_map.120
  (3 shorter events, 0.0 us)
Async XLA Ops:
  1.3 35.0 %copy-start = (bf16[64,64,128]{2,1,0:T(8,128)(2,1)S(1)}, bf16[64,64,128]{2,1,0:T(8,128)(2,1)}, u32[]{:S(2)}) copy-start(bf16[64,64,128]{2,1,0:T(8,128)(2,1)} %local_inverse.1) | copy-start | bytes 3145732
  1.3 35.0 %copy-start.3 = (f32[64,128]{1,0:T(8,128)S(1)}, f32[64,128]{1,0:T(8,128)}, u32[]{:S(2)}) copy-start(f32[64,128]{1,0:T(8,128)} %field.3) | copy-start | bytes 98308
  5.3 30.9 %collective-permute-start.1 = (f32[64,16,128]{2,1,0:T(8,128)}, f32[64,16,128]{2,1,0:T(8,128)S(1)}, u32[]{:S(2)}, u32[]{:S(2)}) collective-permute-start(f32[64,16,128]{2,1,0:T(8,128)} %get-tuple-element.58), channel_id=1, source_target_pairs={{0,8},{1,9},{2,10},{3,11},{8,16},{9,17},{10,18},{11,19},{12,4},{13... | collective-permute-start | bytes 1572872 | tf_op jit(solution)/shard_map/ppermute | solution.py:482
  34.9 2.8 %collective-permute-start = (f32[128,128]{1,0:T(8,128)S(1)}, f32[128,128]{1,0:T(8,128)S(1)}, u32[]{:S(2)}, u32[]{:S(2)}) collective-permute-start(f32[128,128]{1,0:T(8,128)S(1)} %bitcast.16), channel_id=1, source_target_pairs={{0,8},{8,0},{1,9},{9,1},{2,10},{10,2},{3,11},{11,3},{4,12},{12,4},... | collective-permute-start | bytes 196616 | tf_op jit(solution)/shard_map/ppermute | solution.py:451
  36.3 0.7 copy-start.5
  37.0 1.2 copy-start.1
  37.0 1.4 copy-start.2
  37.0 21.5 %slice-start = ((s8[7340032]{0:T(1024)(128)(4,1)}), s8[4194304]{0:T(1024)(128)(4,1)S(1)}, s32[]{:S(2)}) async-start(s8[7340032]{0:T(1024)(128)(4,1)} %bitcast.25), calls=%async_computation.6 | async-start | bytes 8388608
  38.3 20.2 %slice-start.1 = ((s8[7340032]{0:T(1024)(128)(4,1)}), s8[3145728]{0:T(1024)(128)(4,1)S(1)}, s32[]{:S(2)}) async-start(s8[7340032]{0:T(1024)(128)(4,1)} %bitcast.25), calls=%async_computation.7 | async-start | bytes 6291456
  38.3 20.2 %copy-start.4 = (s32[7,128]{1,0:T(8,128)S(1)}, s32[7,128]{1,0:T(8,128)}, u32[]{:S(2)}) copy-start(s32[7,128]{1,0:T(8,128)} %columns.3) | copy-start | bytes 10756
  38.9 5.1 %collective-permute-start.2 = (f32[16,128]{1,0:T(8,128)S(1)}, f32[16,128]{1,0:T(8,128)S(1)}, u32[]{:S(2)}, u32[]{:S(2)}) collective-permute-start(f32[16,128]{1,0:T(8,128)S(1)} %get-tuple-element.61), channel_id=1, source_target_pairs={{4,12},{5,13},{6,14},{7,15},{8,0},{9,1},{10,2},{11,3},{12,20},{13,... | collective-permute-start | bytes 24584 | tf_op jit(solution)/shard_map/ppermute | solution.py:454
  78.4 2.8 %collective-permute-start.3 = (f32[128,128]{1,0:T(8,128)S(1)}, f32[128,128]{1,0:T(8,128)S(1)}, u32[]{:S(2)}, u32[]{:S(2)}) collective-permute-start(f32[128,128]{1,0:T(8,128)S(1)} %bitcast.18), channel_id=1, source_target_pairs={{0,8},{8,0},{1,9},{9,1},{2,10},{10,2},{3,11},{11,3},{4,12},{12,4},... | collective-permute-start | bytes 196616 | tf_op jit(solution)/shard_map/ppermute | solution.py:451
  81.8 5.0 %collective-permute-start.4 = (f32[16,128]{1,0:T(8,128)S(1)}, f32[16,128]{1,0:T(8,128)S(1)}, u32[]{:S(2)}, u32[]{:S(2)}) collective-permute-start(f32[16,128]{1,0:T(8,128)S(1)} %get-tuple-element.69), channel_id=1, source_target_pairs={{4,12},{5,13},{6,14},{7,15},{8,0},{9,1},{10,2},{11,3},{12,20},{13,... | collective-permute-start | bytes 24584 | tf_op jit(solution)/shard_map/ppermute | solution.py:454
  121.3 2.6 %collective-permute-start.5 = (f32[128,128]{1,0:T(8,128)S(1)}, f32[128,128]{1,0:T(8,128)S(1)}, u32[]{:S(2)}, u32[]{:S(2)}) collective-permute-start(f32[128,128]{1,0:T(8,128)S(1)} %bitcast.20), channel_id=1, source_target_pairs={{0,8},{8,0},{1,9},{9,1},{2,10},{10,2},{3,11},{11,3},{4,12},{12,4},... | collective-permute-start | bytes 196616 | tf_op jit(solution)/shard_map/ppermute | solution.py:451
  124.9 10.8 %all-to-all-start.5 = ((f32[32,1,128]{2,1,0:T(1,128)}), f32[32,1,128]{2,1,0:T(1,128)S(1)}, u32[]{:S(2)}, u32[]{:S(2)}) async-start(f32[32,1,128]{2,1,0:T(1,128)} %bitcast.10), calls=%async_computation.5 | async-start | bytes 32768 | tf_op jit(solution)/shard_map/all_to_all | solution.py:447

commit v4 on v3

--- a/solution.py
+++ b/solution.py
@@ -65,11 +65,13 @@
     return jnp.sum(a * b, axis=0, keepdims=True)
 
 
-def project_into(sums_ref, basis_ref, vector):
+def project_into(sums_ref, basis_ref, vector, copy_of=None):
     modes, size, _ = basis_ref.shape
 
     def eight(step, carry):
         first = pl.multiple_of(step * 8, 8)
+        if copy_of:
+            copy_of(step).wait()
         parts = []
         for r in range(8):
             acc = jnp.zeros((16, LANES), F32)
@@ -116,15 +118,18 @@
         table_ref[8 * m : 8 * m + 8, :] = row
 
 
+def own_face(margin_rows, groups):
+    face = jnp.where(lax.axis_index("grp") < groups // 2, 0, 1)
+    return face, jnp.where(face == 0, margin_rows[0, 0:1, :], margin_rows[0, 1:2, :])
+
+
 def begin_body(
-    margin_rows,
     counts,
     field_hbm,
     basis_hbm,
     margin_hbm,
     table,
     packed,
-    meta,
     sums,
     field,
     basis,
@@ -132,34 +137,25 @@
     sems,
     *,
     groups,
-    rows,
+    width,
 ):
-    pairs = [(field_hbm, field), (basis_hbm, basis), (margin_hbm, margin)]
-    copies = [pltpu.make_async_copy(a, b, sems.at[i]) for i, (a, b) in enumerate(pairs)]
-    for copy in copies:
-        copy.start()
-    size = field.shape[0]
-    width = margin_rows.shape[2]
-    group = lax.axis_index("grp")
-    face = jnp.where(group < groups // 2, 0, 1)
-    lane = lane_index(1)
-    slot, owned = jnp.zeros((1, LANES), I32), jnp.zeros((1, LANES), I32)
-    source = jnp.full((1, LANES), -1, I32)
-    for t in range(width):
-        row = margin_rows[0, face, t] - group * rows
-        hit = lane == row
-        slot = jnp.where(hit, t, slot)
-        owned = jnp.where(hit, 1, owned)
-        source = jnp.where(lane % width == t, row, source)
-    inside = ((source >= 0) & (source < rows)).astype(I32)
-    source = jnp.clip(source, 0, rows - 1)
-    meta[...] = jnp.concatenate([slot, owned, source, inside, jnp.zeros((4, LANES), I32)], axis=0)
-
-    copies[0].wait()
-    copies[1].wait()
-    project_into(sums, basis, field[...])
-    write_table(table, sums, counts[0], basis.shape[0], [])
-    copies[2].wait()
+    size, modes = field.shape[0], basis.shape[0]
+
+    def copy_of(step):
+        part = pl.ds(pl.multiple_of(step * 8, 8), 8)
+        return pltpu.make_async_copy(basis_hbm.at[part], basis.at[part], sems.at[step])
+
+    field_copy = pltpu.make_async_copy(field_hbm, field, sems.at[modes // 8])
+    margin_copy = pltpu.make_async_copy(margin_hbm, margin, sems.at[modes // 8 + 1])
+    field_copy.start()
+    for step in range(modes // 8):
+        copy_of(step).start()
+    margin_copy.start()
+    face = jnp.where(lax.axis_index("grp") < groups // 2, 0, 1)
+    field_copy.wait()
+    project_into(sums, basis, field[...], copy_of)
+    write_table(table, sums, counts[0], modes, [])
+    margin_copy.wait()
     parts = LANES // width
     depth = size // parts
     given = lax.broadcasted_iota(I32, (margin.shape[2], LANES), 0)
@@ -173,10 +169,21 @@
     packed[...] = result.reshape(size, depth, LANES)
 
 
-def inverse_body(meta, local_inverse, packed, field, inverse, solved, *, width):
+def inverse_body(margin_rows, local_inverse, packed, field, inverse, solved, *, width, groups):
     size, depth, _ = packed.shape
+    rows = field.shape[1]
+    _, named = own_face(margin_rows, groups)
+    square = (width, width)
+    diagonal = lax.broadcasted_iota(I32, square, 0) == lax.broadcasted_iota(I32, square, 1)
+    owner = jnp.dot(
+        jnp.where(diagonal, named.astype(F32), 0.0),
+        jnp.ones((width, LANES), F32),
+        precision=precise,
+        preferred_element_type=F32,
+    ).astype(I32)
+    owner = jnp.concatenate([owner] * (LANES // width), axis=0)
     row = lax.broadcasted_iota(I32, (LANES, LANES), 0)
-    place = (row % width == meta[0:1, :]) & (meta[1:2, :] > 0)
+    place = owner == lane_index(LANES) + lax.axis_index("grp") * rows
     blocks = packed[...].reshape(size * depth, LANES).astype(jnp.bfloat16)
     for a in range(size // depth):
         chosen = (place & (row // width == a)).astype(F32).astype(jnp.bfloat16)
@@ -237,11 +244,14 @@
     return jnp.broadcast_to(row[:, lane : lane + 1], (1, LANES))
 
 
-def send_out(vector, meta, rim, send, *, width):
-    size = vector.shape[0]
+def send_out(vector, margin_rows, rim, send, *, width):
+    size, rows = vector.shape
     depth = rim.shape[0]
-    picked = pick_lanes(vector, meta[2:3, :])
-    picked = jnp.where(jnp.broadcast_to(meta[3:4, :], picked.shape) > 0, picked, 0.0)
+    _, named = own_face(margin_rows, send.shape[0])
+    named = jnp.concatenate([named] * (LANES // width), axis=1) - lax.axis_index("grp") * rows
+    inside = ((named >= 0) & (named < rows)).astype(I32)
+    picked = pick_lanes(vector, jnp.clip(named, 0, rows - 1))
+    picked = jnp.where(jnp.broadcast_to(inside, picked.shape) > 0, picked, 0.0)
     lanes = lane_index(depth)
     result = jnp.zeros((depth, LANES), F32)
     for a in range(size // depth):
@@ -254,12 +264,25 @@
 
 
 def first_body(
-    counts, table, other, coarse, basis, solved, meta, search, mine, rim, send, weights, *, width
+    counts,
+    table,
+    other,
+    coarse,
+    basis,
+    solved,
+    margin_rows,
+    search,
+    mine,
+    rim,
+    send,
+    weights,
+    *,
+    width,
 ):
     coarse_weights(weights, table, other, coarse, counts[0])
     mine[...] = jnp.broadcast_to(own_row(table), (8, LANES))
     search[...] = solved[...] + expand(weights, basis)
-    send_out(search[...], meta, rim, send, width=width)
+    send_out(search[...], margin_rows, rim, send, width=width)
 
 
 def second_body(
@@ -269,7 +292,7 @@
     coarse,
     basis,
     solved,
-    meta,
+    margin_rows,
     field,
     search,
     image,
@@ -296,7 +319,7 @@
     answer[...] = solved[...] + expand(weights, basis)
     residual[...] = field[...] - step * image[...]
     search1[...] = search[...] - step * answer[...]
-    send_out(search1[...], meta, rim, send, width=width)
+    send_out(search1[...], margin_rows, rim, send, width=width)
 
 
 def pick_columns(got, columns, own, picked, width):
@@ -462,21 +485,20 @@
     weights_of = pltpu.VMEM((modes, LANES), F32)
     picked = pltpu.VMEM((columns.shape[0], size, LANES), F32)
 
-    table, packed, meta = call(
+    table, packed = call(
         begin_body,
-        [table_of, ((size, depth, LANES), F32), ((8, LANES), I32)],
-        [SMEM] * 2 + [HBM] * 3,
-        margin_rows,
+        [table_of, ((size, depth, LANES), F32)],
+        [SMEM] + [HBM] * 3,
         counts,
         right_side,
         basis,
         margin_inverse,
         scratch=[sums]
         + [pltpu.VMEM(x.shape, x.dtype) for x in (right_side, basis, margin_inverse)]
-        + [pltpu.SemaphoreType.DMA((3,))],
+        + [pltpu.SemaphoreType.DMA((modes // 8 + 2,))],
         vmem=62,
         groups=groups,
-        rows=rows,
+        width=width,
     )
     table, other = share(table)
     packed = lax.ppermute(packed, AXES, pairs(1))
@@ -484,11 +506,12 @@
         inverse_body,
         [((size, size, rows), F32), field],
         [VMEM] * 4,
-        meta,
+        margin_rows,
         local_inverse,
         packed,
         right_side,
         width=width,
+        groups=groups,
     )
     z0, mine, rim, send = call(
         first_body,
@@ -500,7 +523,7 @@
         coarse_inverse,
         basis,
         solved,
-        meta,
+        margin_rows,
         scratch=[weights_of],
         width=width,
     )
@@ -533,7 +556,7 @@
         coarse_inverse,
         basis,
         solved,
-        meta,
+        margin_rows,
         right_side,
         z0,
         q0,

time: 137 us -> 135 us (0.985)
  no operation moved by 1% of the time
where the time goes in v4:
time: 135 us
  blocking collectives  88.4 us (65%)
  starting transfers between devices  17.8 us (13%)
  Pallas kernels  13.5 us (10%)
  waiting for transfers between devices  13.3 us (10%)
  between operations  1.41 us (1%)
    all_to_all x3, blocking collectives, exchange(): lax.all_to_all(table.reshape(peers, 1, LANES), axes, 0, 0)  58.7 us
    all_to_all x2, blocking collectives, gather(): return lax.all_to_all(send, 'grp', 0, 0)  29.7 us
    pallas_call x9, Pallas kernels, call(): pl.pallas_call(functools.partial(body, **static), out_shape=shapes, in_sp...  13.5 us
    all_to_all x1, waiting for transfers between devices, exchange(): lax.all_to_all(table.reshape(peers, 1, LANES), axes, 0, 0)  6.13 us
    ppermute x2, waiting for transfers between devices, gather(): rim = lax.ppermute(rim, AXES, pairs(-1))  5.32 us
    ppermute x3, starting transfers between devices, share(): return (table, lax.ppermute(table, 'core', ((0, 1), (1, 0))))  4.75 us
    ppermute x2, starting transfers between devices, gather(): rim = lax.ppermute(rim, AXES, pairs(-1))  4.73 us
    ppermute x1, starting transfers between devices, local(): packed = lax.ppermute(packed, AXES, pairs(1))  4.51 us
  transfers between devices with their start and end apart: 7, of which 5 were waited for; matrix products, arithmetic and copies ran while one was open for 0% of the time, Pallas kernels for 1%

profile of v4, /device:TPU:1, one launch (start us, length us, event | category | flops | bytes accessed | tf_op | source)
XLA Modules:
  0.0 134.5 jit_solution(1914057830587737757)
XLA Ops:
  1.3 0.0 copy-start
  1.3 0.0 copy-start.3
  1.3 0.0 copy-start.5
  1.3 3.1 %shard_map.112 = (f32[128,128]{1,0:T(8,128)}, f32[64,16,128]{2,1,0:T(8,128)}) custom-call(s32[1]{0:T(128)S(6)} %copy.18.counts, f32[64,128]{1,0:T(8,128)} %field.3, bf16[64,64,128]{2,1,0:T(8,128)(2,1)} %basis.9, bf16[64,64,64]{2,1,0:T(8,128)(2,1)} %margin_hbm.1), custom_call_target="tpu_custom_call" | custom-call | flops 4000000000 | bytes 1605636 | tf_op jit(solution)/shard_map/pallas_call | solution.py:25
  4.5 4.5 %collective-permute-start.1 = (f32[64,16,128]{2,1,0:T(8,128)}, f32[64,16,128]{2,1,0:T(8,128)S(1)}, u32[]{:S(2)}, u32[]{:S(2)}) collective-permute-start(f32[64,16,128]{2,1,0:T(8,128)} %get-tuple-element.56), channel_id=1, source_target_pairs={{0,8},{1,9},{2,10},{3,11},{8,16},{9,17},{10,18},{11,19},{12,4},{13... | collective-permute-start | bytes 1572872 | tf_op jit(solution)/shard_map/ppermute | solution.py:504
  9.0 25.0 %all_to_all.30 = f32[128,1,128]{2,1,0:T(1,128)S(1)} all-to-all(f32[128,1,128]{2,1,0:T(1,128)} %bitcast.27), channel_id=1, replica_groups=mesh['plane'=16,'core'=2,'grp'=8] {'plane','grp'}, dimensions={0} | all-to-all | bytes 131072 | tf_op jit(solution)/shard_map/all_to_all | solution.py:470
  34.0 0.0 copy-start.1
  34.0 0.0 copy-start.2
  34.0 1.4 %collective-permute-start = (f32[128,128]{1,0:T(8,128)S(1)}, f32[128,128]{1,0:T(8,128)S(1)}, u32[]{:S(2)}, u32[]{:S(2)}) collective-permute-start(f32[128,128]{1,0:T(8,128)S(1)} %bitcast.16), channel_id=1, source_target_pairs={{0,8},{8,0},{1,9},{9,1},{2,10},{10,2},{3,11},{11,3},{4,12},{12,4},... | collective-permute-start | bytes 196616 | tf_op jit(solution)/shard_map/ppermute | solution.py:474
  35.4 0.0 collective-permute-done.1.packed
  35.4 0.0 copy-done
  35.4 0.0 copy-done.3
  35.4 0.0 copy-done.5
  35.4 0.0 slice-start
  35.4 0.8 shard_map.113
  36.3 0.0 collective-permute-done.other
  36.3 0.0 copy-done.1
  36.3 0.0 copy-done.2
  36.3 0.0 slice-start.1
  36.3 0.0 copy-start.4
  36.3 0.7 shard_map.114
  37.0 2.5 %collective-permute-start.2 = (f32[16,128]{1,0:T(8,128)S(1)}, f32[16,128]{1,0:T(8,128)S(1)}, u32[]{:S(2)}, u32[]{:S(2)}) collective-permute-start(f32[16,128]{1,0:T(8,128)S(1)} %get-tuple-element.59), channel_id=1, source_target_pairs={{4,12},{5,13},{6,14},{7,15},{8,0},{9,1},{10,2},{11,3},{12,20},{13,... | collective-permute-start | bytes 24584 | tf_op jit(solution)/shard_map/ppermute | solution.py:477
  39.5 2.6 %collective-permute-done.2 = f32[16,128]{1,0:T(8,128)S(1)} collective-permute-done((f32[16,128]{1,0:T(8,128)S(1)}, f32[16,128]{1,0:T(8,128)S(1)}, u32[]{:S(2)}, u32[]{:S(2)}) %collective-permute-start.2) | collective-permute-done | bytes 8224 | tf_op jit(solution)/shard_map/ppermute | solution.py:477
  42.1 14.9 %all_to_all.31.got = f32[8,80,128]{2,1,0:T(8,128)S(1)} all-to-all(f32[8,80,128]{2,1,0:T(8,128)S(1)} %broadcast_dynamic-update-slice_fusion.1), channel_id=1, replica_groups=mesh['plane'=16,'core'=2,'grp'=8] {'grp'}, dimensions={0} | all-to-all | bytes 655360 | tf_op jit(solution)/shard_map/all_to_all | solution.py:479
  57.0 0.0 slice-done
  57.0 0.0 slice-done.1
  57.0 0.0 copy-done.4
  57.0 2.8 %shard_map.115 = (f32[64,128]{1,0:T(8,128)S(1)}, f32[64,128]{1,0:T(8,128)S(1)}, f32[128,128]{1,0:T(8,128)S(1)}) custom-call(s32[1]{0:T(128)S(6)} %copy.18.counts, f32[8,80,128]{2,1,0:T(8,128)S(1)} %all_to_all.31.got, s32[7,128]{1,0:T(8,128)S(1)} %copy-done.4, bf16[7,64,64,128]{3,2,1,0:T(8,128)(2,1)S(1)} %bitcast.26, bf16[64,64,128]{2,1,0:T(8,128)(2,1)S(1)} %copy-done.1, ...), custom_call_target="tpu_custom_call" | custom-call | flops 4000000000 | bytes 10882564 | tf_op jit(solution)/shard_map/pallas_call | solution.py:25
  59.8 16.9 %all_to_all.32 = f32[128,1,128]{2,1,0:T(1,128)S(1)} all-to-all(f32[128,1,128]{2,1,0:T(1,128)S(1)} %bitcast.23), channel_id=1, replica_groups=mesh['plane'=16,'core'=2,'grp'=8] {'plane','grp'}, dimensions={0} | all-to-all | bytes 131072 | tf_op jit(solution)/shard_map/all_to_all | solution.py:470
  76.7 1.7 %collective-permute-start.3 = (f32[128,128]{1,0:T(8,128)S(1)}, f32[128,128]{1,0:T(8,128)S(1)}, u32[]{:S(2)}, u32[]{:S(2)}) collective-permute-start(f32[128,128]{1,0:T(8,128)S(1)} %bitcast.18), channel_id=1, source_target_pairs={{0,8},{8,0},{1,9},{9,1},{2,10},{10,2},{3,11},{11,3},{4,12},{12,4},... | collective-permute-start | bytes 196616 | tf_op jit(solution)/shard_map/ppermute | solution.py:474
  78.4 0.9 collective-permute-done.3.other
  79.3 0.7 shard_map.116
  80.0 2.3 %collective-permute-start.4 = (f32[16,128]{1,0:T(8,128)S(1)}, f32[16,128]{1,0:T(8,128)S(1)}, u32[]{:S(2)}, u32[]{:S(2)}) collective-permute-start(f32[16,128]{1,0:T(8,128)S(1)} %get-tuple-element.67), channel_id=1, source_target_pairs={{4,12},{5,13},{6,14},{7,15},{8,0},{9,1},{10,2},{11,3},{12,20},{13,... | collective-permute-start | bytes 24584 | tf_op jit(solution)/shard_map/ppermute | solution.py:477
  82.2 2.7 %collective-permute-done.4 = f32[16,128]{1,0:T(8,128)S(1)} collective-permute-done((f32[16,128]{1,0:T(8,128)S(1)}, f32[16,128]{1,0:T(8,128)S(1)}, u32[]{:S(2)}, u32[]{:S(2)}) %collective-permute-start.4) | collective-permute-done | bytes 8224 | tf_op jit(solution)/shard_map/ppermute | solution.py:477
  84.9 14.8 %all_to_all.33.got = f32[8,80,128]{2,1,0:T(8,128)S(1)} all-to-all(f32[8,80,128]{2,1,0:T(8,128)S(1)} %broadcast_dynamic-update-slice_fusion), channel_id=1, replica_groups=mesh['plane'=16,'core'=2,'grp'=8] {'grp'}, dimensions={0} | all-to-all | bytes 655360 | tf_op jit(solution)/shard_map/all_to_all | solution.py:479
  99.7 2.8 %shard_map.117 = (f32[64,128]{1,0:T(8,128)S(1)}, f32[64,128]{1,0:T(8,128)S(1)}, f32[128,128]{1,0:T(8,128)S(1)}) custom-call(s32[1]{0:T(128)S(6)} %copy.18.counts, f32[8,80,128]{2,1,0:T(8,128)S(1)} %all_to_all.33.got, s32[7,128]{1,0:T(8,128)S(1)} %copy-done.4, bf16[7,64,64,128]{3,2,1,0:T(8,128)(2,1)S(1)} %bitcast.26, bf16[64,64,128]{2,1,0:T(8,128)(2,1)S(1)} %copy-done.1, ...), custom_call_target="tpu_custom_call" | custom-call | flops 4000000000 | bytes 10980868 | tf_op jit(solution)/shard_map/pallas_call | solution.py:25
  102.6 16.9 %all_to_all.34 = f32[128,1,128]{2,1,0:T(1,128)S(1)} all-to-all(f32[128,1,128]{2,1,0:T(1,128)S(1)} %bitcast.22), channel_id=1, replica_groups=mesh['plane'=16,'core'=2,'grp'=8] {'plane','grp'}, dimensions={0} | all-to-all | bytes 131072 | tf_op jit(solution)/shard_map/all_to_all | solution.py:470
  119.4 1.7 %collective-permute-start.5 = (f32[128,128]{1,0:T(8,128)S(1)}, f32[128,128]{1,0:T(8,128)S(1)}, u32[]{:S(2)}, u32[]{:S(2)}) collective-permute-start(f32[128,128]{1,0:T(8,128)S(1)} %bitcast.20), channel_id=1, source_target_pairs={{0,8},{8,0},{1,9},{9,1},{2,10},{10,2},{3,11},{11,3},{4,12},{12,4},... | collective-permute-start | bytes 196616 | tf_op jit(solution)/shard_map/ppermute | solution.py:474
  121.1 0.9 collective-permute-done.5.other
  122.0 1.1 shard_map.118
  123.1 3.8 %all-to-all-start.5 = ((f32[32,1,128]{2,1,0:T(1,128)}), f32[32,1,128]{2,1,0:T(1,128)S(1)}, u32[]{:S(2)}, u32[]{:S(2)}) async-start(f32[32,1,128]{2,1,0:T(1,128)} %bitcast.10), calls=%async_computation.5 | async-start | bytes 32768 | tf_op jit(solution)/shard_map/all_to_all | solution.py:470
  126.9 0.8 shard_map.119
  127.8 6.1 %all-to-all-done.5 = f32[32,1,128]{2,1,0:T(1,128)S(1)} async-done(((f32[32,1,128]{2,1,0:T(1,128)}), f32[32,1,128]{2,1,0:T(1,128)S(1)}, u32[]{:S(2)}, u32[]{:S(2)}) %all-to-all-start.5) | async-done | bytes 16416 | tf_op jit(solution)/shard_map/all_to_all | solution.py:470
  133.9 0.6 shard_map.120
  (3 shorter events, 0.0 us)
Async XLA Ops:
  1.3 34.1 %copy-start = (bf16[64,64,128]{2,1,0:T(8,128)(2,1)S(1)}, bf16[64,64,128]{2,1,0:T(8,128)(2,1)}, u32[]{:S(2)}) copy-start(bf16[64,64,128]{2,1,0:T(8,128)(2,1)} %local_inverse.1) | copy-start | bytes 3145732
  1.3 34.1 %copy-start.3 = (f32[64,128]{1,0:T(8,128)S(1)}, f32[64,128]{1,0:T(8,128)}, u32[]{:S(2)}) copy-start(f32[64,128]{1,0:T(8,128)} %field.3) | copy-start | bytes 98308
  1.3 34.1 %copy-start.5 = (s32[1,2,32]{2,1,0:T(2,128)S(1)}, s32[1,2,32]{2,1,0:T(2,128)}, u32[]{:S(2)}) copy-start(s32[1,2,32]{2,1,0:T(2,128)} %margin_rows.5) | copy-start | bytes 772
  4.5 31.0 %collective-permute-start.1 = (f32[64,16,128]{2,1,0:T(8,128)}, f32[64,16,128]{2,1,0:T(8,128)S(1)}, u32[]{:S(2)}, u32[]{:S(2)}) collective-permute-start(f32[64,16,128]{2,1,0:T(8,128)} %get-tuple-element.56), channel_id=1, source_target_pairs={{0,8},{1,9},{2,10},{3,11},{8,16},{9,17},{10,18},{11,19},{12,4},{13... | collective-permute-start | bytes 1572872 | tf_op jit(solution)/shard_map/ppermute | solution.py:504
  34.0 2.3 %copy-start.1 = (bf16[64,64,128]{2,1,0:T(8,128)(2,1)S(1)}, bf16[64,64,128]{2,1,0:T(8,128)(2,1)}, u32[]{:S(2)}) copy-start(bf16[64,64,128]{2,1,0:T(8,128)(2,1)} %basis.9) | copy-start | bytes 3145732
  34.0 2.3 %copy-start.2 = (f32[64,2048]{1,0:T(8,128)S(1)}, f32[64,2048]{1,0:T(8,128)}, u32[]{:S(2)}) copy-start(f32[64,2048]{1,0:T(8,128)} %coarse.5) | copy-start | bytes 1572868
  34.0 2.3 %collective-permute-start = (f32[128,128]{1,0:T(8,128)S(1)}, f32[128,128]{1,0:T(8,128)S(1)}, u32[]{:S(2)}, u32[]{:S(2)}) collective-permute-start(f32[128,128]{1,0:T(8,128)S(1)} %bitcast.16), channel_id=1, source_target_pairs={{0,8},{8,0},{1,9},{9,1},{2,10},{10,2},{3,11},{11,3},{4,12},{12,4},... | collective-permute-start | bytes 196616 | tf_op jit(solution)/shard_map/ppermute | solution.py:474
  35.4 21.6 %slice-start = ((s8[7340032]{0:T(1024)(128)(4,1)}), s8[4194304]{0:T(1024)(128)(4,1)S(1)}, s32[]{:S(2)}) async-start(s8[7340032]{0:T(1024)(128)(4,1)} %bitcast.25), calls=%async_computation.6 | async-start | bytes 8388608
  36.3 20.7 %slice-start.1 = ((s8[7340032]{0:T(1024)(128)(4,1)}), s8[3145728]{0:T(1024)(128)(4,1)S(1)}, s32[]{:S(2)}) async-start(s8[7340032]{0:T(1024)(128)(4,1)} %bitcast.25), calls=%async_computation.7 | async-start | bytes 6291456
  36.3 20.7 %copy-start.4 = (s32[7,128]{1,0:T(8,128)S(1)}, s32[7,128]{1,0:T(8,128)}, u32[]{:S(2)}) copy-start(s32[7,128]{1,0:T(8,128)} %columns.3) | copy-start | bytes 10756
  37.0 5.1 %collective-permute-start.2 = (f32[16,128]{1,0:T(8,128)S(1)}, f32[16,128]{1,0:T(8,128)S(1)}, u32[]{:S(2)}, u32[]{:S(2)}) collective-permute-start(f32[16,128]{1,0:T(8,128)S(1)} %get-tuple-element.59), channel_id=1, source_target_pairs={{4,12},{5,13},{6,14},{7,15},{8,0},{9,1},{10,2},{11,3},{12,20},{13,... | collective-permute-start | bytes 24584 | tf_op jit(solution)/shard_map/ppermute | solution.py:477
  76.7 2.6 %collective-permute-start.3 = (f32[128,128]{1,0:T(8,128)S(1)}, f32[128,128]{1,0:T(8,128)S(1)}, u32[]{:S(2)}, u32[]{:S(2)}) collective-permute-start(f32[128,128]{1,0:T(8,128)S(1)} %bitcast.18), channel_id=1, source_target_pairs={{0,8},{8,0},{1,9},{9,1},{2,10},{10,2},{3,11},{11,3},{4,12},{12,4},... | collective-permute-start | bytes 196616 | tf_op jit(solution)/shard_map/ppermute | solution.py:474
  80.0 5.0 %collective-permute-start.4 = (f32[16,128]{1,0:T(8,128)S(1)}, f32[16,128]{1,0:T(8,128)S(1)}, u32[]{:S(2)}, u32[]{:S(2)}) collective-permute-start(f32[16,128]{1,0:T(8,128)S(1)} %get-tuple-element.67), channel_id=1, source_target_pairs={{4,12},{5,13},{6,14},{7,15},{8,0},{9,1},{10,2},{11,3},{12,20},{13,... | collective-permute-start | bytes 24584 | tf_op jit(solution)/shard_map/ppermute | solution.py:477
  119.4 2.6 %collective-permute-start.5 = (f32[128,128]{1,0:T(8,128)S(1)}, f32[128,128]{1,0:T(8,128)S(1)}, u32[]{:S(2)}, u32[]{:S(2)}) collective-permute-start(f32[128,128]{1,0:T(8,128)S(1)} %bitcast.20), channel_id=1, source_target_pairs={{0,8},{8,0},{1,9},{9,1},{2,10},{10,2},{3,11},{11,3},{4,12},{12,4},... | collective-permute-start | bytes 196616 | tf_op jit(solution)/shard_map/ppermute | solution.py:474
  123.1 10.8 %all-to-all-start.5 = ((f32[32,1,128]{2,1,0:T(1,128)}), f32[32,1,128]{2,1,0:T(1,128)S(1)}, u32[]{:S(2)}, u32[]{:S(2)}) async-start(f32[32,1,128]{2,1,0:T(1,128)} %bitcast.10), calls=%async_computation.5 | async-start | bytes 32768 | tf_op jit(solution)/shard_map/all_to_all | solution.py:470

commit v5 on v4

--- a/solution.py
+++ b/solution.py
@@ -105,14 +105,13 @@
     rest = LANES - modes
     rows = dots + [jnp.zeros((1, LANES), F32)] * (rest - len(dots))
     sums_ref[modes:, :] = jnp.concatenate(rows, axis=0)
-    row = lax.dot_general(
-        jnp.ones((8, LANES), F32),
-        sums_ref[...],
-        (((1,), (1,)), ((), ())),
-        precision=precise,
-        preferred_element_type=F32,
-    )
     lane = lane_index()
+    own = lax.broadcasted_iota(I32, (8, LANES), 0)
+    acc = jnp.zeros((8, LANES), F32)
+    for m in range(0, LANES, 8):
+        value = jnp.sum(sums_ref[m : m + 8, :], axis=1, keepdims=True)
+        acc += jnp.where(lane == own + m, value, 0.0)
+    row = jnp.broadcast_to(jnp.sum(acc, axis=0, keepdims=True), (8, LANES))
     row = jnp.where((lane < count) | (lane >= modes), row, 0.0)
     for m in range(table_ref.shape[0] // 8):
         table_ref[8 * m : 8 * m + 8, :] = row
@@ -195,27 +194,21 @@
 
 def coarse_weights(weights_ref, mine, other, coarse, count):
     modes = coarse.shape[0]
-    lane = lane_index()
+    lane = lane_index(1)
     accs = [jnp.zeros((8, LANES), F32) for _ in range(modes // 8)]
-    totals = jnp.zeros((8, LANES), F32)
+    totals = jnp.zeros((1, LANES), F32)
     first = lax.axis_index("core") == 0
-    for m in range(mine.shape[0] // 8):
-        own, twin = mine[8 * m : 8 * m + 8, :], other[8 * m : 8 * m + 8, :]
+    for m in range(mine.shape[0]):
+        own, twin = mine[m : m + 1, :], other[m : m + 1, :]
         totals += own + twin
         even, odd = jnp.where(first, own, twin), jnp.where(first, twin, own)
         both = jnp.where(lane < modes, even, pltpu.roll(odd, modes, 1))
-        both = jnp.sum(both, axis=0, keepdims=True)
         for r in range(modes // 8):
             accs[r] += coarse[8 * r : 8 * r + 8, LANES * m : LANES * m + LANES] * both
-    weights = jnp.dot(
-        jnp.concatenate(accs, axis=0),
-        jnp.ones((LANES, LANES), F32),
-        precision=precise,
-        preferred_element_type=F32,
-    )
+    weights = jnp.sum(jnp.concatenate(accs, axis=0), axis=1, keepdims=True)
     rows = lax.broadcasted_iota(I32, (modes, LANES), 0)
     weights_ref[...] = jnp.where(rows < count, weights, 0.0)
-    return jnp.sum(totals, axis=0, keepdims=True)
+    return totals
 
 
 def expand(weights_ref, basis):
@@ -236,8 +229,7 @@
 
 
 def own_row(table):
-    start = pl.multiple_of(lax.axis_index("plane") * 8, 8)
-    return jnp.sum(table[pl.ds(start, 8), :], axis=0, keepdims=True)
+    return table[pl.ds(lax.axis_index("plane"), 1), :]
 
 
 def spread(row, lane):
@@ -371,16 +363,26 @@
     lax.fori_loop(0, size // 8, eight, 0)
 
 
-def stiff_body(counts, got, columns, stiffness, basis, inverse, *refs, others, pairs, width):
+def stiff_body(counts, got, columns, stiffness, basis, *refs, others, pairs, width, solve):
     vectors = refs[:others]
-    image, solved, table, picked, sums = refs[others:]
+    refs = refs[others:]
+    if solve:
+        inverse, image, table, solved, picked, sums = refs
+    else:
+        image, table, picked, sums = refs
     pick_columns(got, columns, vectors[0], picked, width)
     stiff_into(image, stiffness, picked)
     project_into(sums, basis, image[...])
-    block_product(solved, inverse, image[...])
-    named = list(vectors) + [image, solved]
+    named = list(vectors) + [image]
+    if solve:
+        block_product(solved, inverse, image[...])
+        named.append(solved)
     dots = [total(named[a][...], named[b][...]) for a, b in pairs]
     write_table(table, sums, counts[0], basis.shape[0], dots)
+
+
+def solve_body(inverse, image, solved):
+    block_product(solved, inverse, image[...])
 
 
 def closing_body(counts, table, other, coarse, scalars, mine, weights, out_table, out_scalars):
@@ -394,11 +396,11 @@
     step = e1 / (z1y1 + beta * (z1q0 + z0y1) + beta * beta * z0q0)
     p_y1 = own_row(table)
     p_q1 = p_y1 + beta * mine[1:2, :]
-    side = jnp.broadcast_to(step * p_q1 - mine[0:1, :], (8, LANES))
-    share = jnp.dot(
-        side[:, :modes], weights[...], precision=precise, preferred_element_type=F32
-    )
-    out_table[...] = jnp.broadcast_to(share[0:1, :], out_table.shape)
+    side = step * p_q1 - mine[0:1, :]
+    place = lax.broadcasted_iota(I32, (modes, LANES), 0) == lane_index(modes)
+    share = jnp.sum(jnp.where(place, weights[...] * side, 0.0), axis=0, keepdims=True)
+    share = jnp.sum(share, axis=1, keepdims=True)
+    out_table[...] = jnp.broadcast_to(share, out_table.shape)
     q1m1 = y1s + beta * (y1m0 + q0s) + beta * beta * q0m0
     known = step * q1m1 - (z1y1 + beta * z1q0) - (r1s + beta * r1m0)
     rows = [e1, beta, step, step0, known, jnp.zeros((3, LANES), F32)]
@@ -470,7 +472,7 @@
         return lax.all_to_all(table.reshape(peers, 1, LANES), axes, 0, 0).reshape(peers, LANES)
 
     def share(table):
-        table = exchange(table, ("plane", "grp"))
+        table = exchange(table, ("plane", "grp")).reshape(planes, groups, LANES).sum(axis=1)
         return table, lax.ppermute(table, "core", ((0, 1), (1, 0)))
 
     def gather(rim, send):
@@ -528,25 +530,27 @@
         width=width,
     )
 
-    def stiff(got, vectors, dots):
+    def stiff(got, vectors, dots, solve):
         return call(
             stiff_body,
-            [field, field, table_of],
-            [SMEM] + [VMEM] * (5 + len(vectors)),
+            [field, table_of] + [field] * solve,
+            [SMEM] + [VMEM] * (4 + len(vectors) + solve),
             counts,
             got,
             columns,
             stiffness,
             basis,
-            inverse,
             *vectors,
+            *[inverse] * solve,
             scratch=[picked, sums],
             others=len(vectors),
             pairs=dots,
             width=width,
+            solve=solve,
         )
 
-    q0, solved, table = stiff(gather(rim, send), [z0, right_side], [(1, 0), (0, 2)])
+    q0, table = stiff(gather(rim, send), [z0, right_side], [(1, 0), (0, 2)], 0)
+    (solved,) = call(solve_body, [field], [VMEM] * 2, inverse, q0)
     m0, r1, z1, mine, scalars, rim, send = call(
         second_body,
         [field, field, field, small, small, rim_of, send_of],
@@ -565,7 +569,7 @@
         width=width,
     )
     dots = [(1, 0), (0, 5), (0, 3), (2, 5), (1, 6), (5, 6), (3, 6), (1, 4), (5, 4), (3, 4)]
-    y1, solved, table = stiff(gather(rim, send), [z1, r1, z0, q0, m0], dots)
+    y1, table, solved = stiff(gather(rim, send), [z1, r1, z0, q0, m0], dots, 1)
     weights, table, scalars = call(
         closing_body,
         [((modes, LANES), F32), ((slabs, LANES), F32), small],

time: 135 us -> 134 us (level)
    pallas_call x9 -> x10, Pallas kernels: 13.5 us -> 12.9 us  [call(): pl.pallas_call(functools.partial(body, **static), out_shape=shapes, in_sp...]
where the time goes in v5:
time: 134 us
  blocking collectives  88.3 us (66%)
  starting transfers between devices  18 us (13%)
  waiting for transfers between devices  13 us (10%)
  Pallas kernels  12.9 us (10%)
  between operations  1.48 us (1%)
    all_to_all x3, blocking collectives, exchange(): lax.all_to_all(table.reshape(peers, 1, LANES), axes, 0, 0)  58.7 us
    all_to_all x2, blocking collectives, gather(): return lax.all_to_all(send, 'grp', 0, 0)  29.6 us
    pallas_call x10, Pallas kernels, call(): pl.pallas_call(functools.partial(body, **static), out_shape=shapes, in_sp...  12.9 us
    all_to_all x1, waiting for transfers between devices, exchange(): lax.all_to_all(table.reshape(peers, 1, LANES), axes, 0, 0)  6.13 us
    ppermute x2, waiting for transfers between devices, gather(): rim = lax.ppermute(rim, AXES, pairs(-1))  5.43 us
    ppermute x3, starting transfers between devices, share(): return (table, lax.ppermute(table, 'core', ((0, 1), (1, 0))))  5.08 us
    ppermute x2, starting transfers between devices, gather(): rim = lax.ppermute(rim, AXES, pairs(-1))  4.62 us
    ppermute x1, starting transfers between devices, local(): packed = lax.ppermute(packed, AXES, pairs(1))  4.51 us
  transfers between devices with their start and end apart: 7, of which 5 were waited for; matrix products, arithmetic and copies ran while one was open for 0% of the time, Pallas kernels for 1%

profile of v5, /device:TPU:1, one launch (start us, length us, event | category | flops | bytes accessed | tf_op | source)
XLA Modules:
  0.0 133.8 jit_solution(14738571340188537495)
XLA Ops:
  1.3 0.0 copy-start
  1.3 0.0 copy-start.3
  1.3 0.0 copy-start.5
  1.3 3.0 %shard_map.112 = (f32[128,128]{1,0:T(8,128)}, f32[64,16,128]{2,1,0:T(8,128)}) custom-call(s32[1]{0:T(128)S(6)} %copy.18.counts, f32[64,128]{1,0:T(8,128)} %field.3, bf16[64,64,128]{2,1,0:T(8,128)(2,1)} %basis.9, bf16[64,64,64]{2,1,0:T(8,128)(2,1)} %margin_hbm.1), custom_call_target="tpu_custom_call" | custom-call | flops 4000000000 | bytes 1605636 | tf_op jit(solution)/shard_map/pallas_call | solution.py:25
  4.3 4.5 %collective-permute-start.1 = (f32[64,16,128]{2,1,0:T(8,128)}, f32[64,16,128]{2,1,0:T(8,128)S(1)}, u32[]{:S(2)}, u32[]{:S(2)}) collective-permute-start(f32[64,16,128]{2,1,0:T(8,128)} %get-tuple-element.55), channel_id=1, source_target_pairs={{0,8},{1,9},{2,10},{3,11},{8,16},{9,17},{10,18},{11,19},{12,4},{13... | collective-permute-start | bytes 1572872 | tf_op jit(solution)/shard_map/ppermute | solution.py:506
  8.9 25.0 %all_to_all.30 = f32[128,1,128]{2,1,0:T(1,128)S(1)} all-to-all(f32[128,1,128]{2,1,0:T(1,128)} %bitcast.30), channel_id=1, replica_groups=mesh['plane'=16,'core'=2,'grp'=8] {'plane','grp'}, dimensions={0} | all-to-all | bytes 131072 | tf_op jit(solution)/shard_map/all_to_all | solution.py:472
  33.9 0.0 copy-start.1
  33.9 0.0 copy-start.2
  33.9 1.5 %collective-permute-start = (f32[16,128]{1,0:T(8,128)S(1)}, f32[16,128]{1,0:T(8,128)S(1)}, u32[]{:S(2)}, u32[]{:S(2)}) collective-permute-start(f32[16,128]{1,0:T(8,128)S(1)} %bitcast_reduce_fusion.2.table), channel_id=1, source_target_pairs={{0,8},{8,0},{1,9},{9,1},{2,10},{10,2},{3,11},{11,3},{4,12},{12,4},... | collective-permute-start | bytes 24584 | tf_op jit(solution)/shard_map/ppermute | solution.py:476
  35.4 0.0 collective-permute-done.1.packed
  35.4 0.0 copy-done
  35.4 0.0 copy-done.3
  35.4 0.0 copy-done.5
  35.4 0.0 slice-start
  35.4 0.8 shard_map.113
  36.3 0.0 collective-permute-done.other
  36.3 0.0 copy-done.1
  36.3 0.0 copy-done.2
  36.3 0.0 slice-start.1
  36.3 0.0 copy-start.4
  36.3 0.6 shard_map.114
  36.9 2.4 %collective-permute-start.2 = (f32[16,128]{1,0:T(8,128)S(1)}, f32[16,128]{1,0:T(8,128)S(1)}, u32[]{:S(2)}, u32[]{:S(2)}) collective-permute-start(f32[16,128]{1,0:T(8,128)S(1)} %get-tuple-element.58), channel_id=1, source_target_pairs={{4,12},{5,13},{6,14},{7,15},{8,0},{9,1},{10,2},{11,3},{12,20},{13,... | collective-permute-start | bytes 24584 | tf_op jit(solution)/shard_map/ppermute | solution.py:479
  39.3 2.7 %collective-permute-done.2 = f32[16,128]{1,0:T(8,128)S(1)} collective-permute-done((f32[16,128]{1,0:T(8,128)S(1)}, f32[16,128]{1,0:T(8,128)S(1)}, u32[]{:S(2)}, u32[]{:S(2)}) %collective-permute-start.2) | collective-permute-done | bytes 8224 | tf_op jit(solution)/shard_map/ppermute | solution.py:479
  42.0 14.8 %all_to_all.31.got = f32[8,80,128]{2,1,0:T(8,128)S(1)} all-to-all(f32[8,80,128]{2,1,0:T(8,128)S(1)} %broadcast_dynamic-update-slice_fusion.1), channel_id=1, replica_groups=mesh['plane'=16,'core'=2,'grp'=8] {'grp'}, dimensions={0} | all-to-all | bytes 655360 | tf_op jit(solution)/shard_map/all_to_all | solution.py:481
  56.8 0.0 slice-done
  56.8 0.0 slice-done.1
  56.8 0.0 copy-done.4
  56.9 2.5 %shard_map.115 = (f32[64,128]{1,0:T(8,128)S(1)}, f32[128,128]{1,0:T(8,128)S(1)}) custom-call(s32[1]{0:T(128)S(6)} %copy.18.counts, f32[8,80,128]{2,1,0:T(8,128)S(1)} %all_to_all.31.got, s32[7,128]{1,0:T(8,128)S(1)} %copy-done.4, bf16[7,64,64,128]{3,2,1,0:T(8,128)(2,1)S(1)} %bitcast.26, bf16[64,64,128]{2,1,0:T(8,128)(2,1)S(1)} %copy-done.1, ...), custom_call_target="tpu_custom_call" | custom-call | flops 4000000000 | bytes 8785412 | tf_op jit(solution)/shard_map/pallas_call | solution.py:25
  59.3 16.9 %all_to_all.32 = f32[128,1,128]{2,1,0:T(1,128)S(1)} all-to-all(f32[128,1,128]{2,1,0:T(1,128)S(1)} %bitcast.23), channel_id=1, replica_groups=mesh['plane'=16,'core'=2,'grp'=8] {'plane','grp'}, dimensions={0} | all-to-all | bytes 131072 | tf_op jit(solution)/shard_map/all_to_all | solution.py:472
  76.2 1.8 %collective-permute-start.3 = (f32[16,128]{1,0:T(8,128)S(1)}, f32[16,128]{1,0:T(8,128)S(1)}, u32[]{:S(2)}, u32[]{:S(2)}) collective-permute-start(f32[16,128]{1,0:T(8,128)S(1)} %bitcast_reduce_fusion.1.table), channel_id=1, source_target_pairs={{0,8},{8,0},{1,9},{9,1},{2,10},{10,2},{3,11},{11,3},{4,12},{12,4},... | collective-permute-start | bytes 24584 | tf_op jit(solution)/shard_map/ppermute | solution.py:476
  78.0 0.2 shard_map.116.solved
  78.3 0.6 collective-permute-done.3.other
  78.9 0.6 shard_map.117
  79.5 2.3 %collective-permute-start.4 = (f32[16,128]{1,0:T(8,128)S(1)}, f32[16,128]{1,0:T(8,128)S(1)}, u32[]{:S(2)}, u32[]{:S(2)}) collective-permute-start(f32[16,128]{1,0:T(8,128)S(1)} %get-tuple-element.65), channel_id=1, source_target_pairs={{4,12},{5,13},{6,14},{7,15},{8,0},{9,1},{10,2},{11,3},{12,20},{13,... | collective-permute-start | bytes 24584 | tf_op jit(solution)/shard_map/ppermute | solution.py:479
  81.7 2.7 %collective-permute-done.4 = f32[16,128]{1,0:T(8,128)S(1)} collective-permute-done((f32[16,128]{1,0:T(8,128)S(1)}, f32[16,128]{1,0:T(8,128)S(1)}, u32[]{:S(2)}, u32[]{:S(2)}) %collective-permute-start.4) | collective-permute-done | bytes 8224 | tf_op jit(solution)/shard_map/ppermute | solution.py:479
  84.4 14.8 %all_to_all.33.got = f32[8,80,128]{2,1,0:T(8,128)S(1)} all-to-all(f32[8,80,128]{2,1,0:T(8,128)S(1)} %broadcast_dynamic-update-slice_fusion), channel_id=1, replica_groups=mesh['plane'=16,'core'=2,'grp'=8] {'grp'}, dimensions={0} | all-to-all | bytes 655360 | tf_op jit(solution)/shard_map/all_to_all | solution.py:481
  99.3 2.7 %shard_map.118 = (f32[64,128]{1,0:T(8,128)S(1)}, f32[128,128]{1,0:T(8,128)S(1)}, f32[64,128]{1,0:T(8,128)S(1)}) custom-call(s32[1]{0:T(128)S(6)} %copy.18.counts, f32[8,80,128]{2,1,0:T(8,128)S(1)} %all_to_all.33.got, s32[7,128]{1,0:T(8,128)S(1)} %copy-done.4, bf16[7,64,64,128]{3,2,1,0:T(8,128)(2,1)S(1)} %bitcast.26, bf16[64,64,128]{2,1,0:T(8,128)(2,1)S(1)} %copy-done.1, ...), custom_call_target="tpu_custom_call" | custom-call | flops 4000000000 | bytes 10980868 | tf_op jit(solution)/shard_map/pallas_call | solution.py:25
  102.0 16.8 %all_to_all.34 = f32[128,1,128]{2,1,0:T(1,128)S(1)} all-to-all(f32[128,1,128]{2,1,0:T(1,128)S(1)} %bitcast.22), channel_id=1, replica_groups=mesh['plane'=16,'core'=2,'grp'=8] {'plane','grp'}, dimensions={0} | all-to-all | bytes 131072 | tf_op jit(solution)/shard_map/all_to_all | solution.py:472
  118.9 1.8 %collective-permute-start.5 = (f32[16,128]{1,0:T(8,128)S(1)}, f32[16,128]{1,0:T(8,128)S(1)}, u32[]{:S(2)}, u32[]{:S(2)}) collective-permute-start(f32[16,128]{1,0:T(8,128)S(1)} %bitcast_reduce_fusion.table), channel_id=1, source_target_pairs={{0,8},{8,0},{1,9},{9,1},{2,10},{10,2},{3,11},{11,3},{4,12},{12,4},... | collective-permute-start | bytes 24584 | tf_op jit(solution)/shard_map/ppermute | solution.py:476
  120.6 0.8 collective-permute-done.5.other
  121.5 0.9 shard_map.119
  122.3 3.8 %all-to-all-start.5 = ((f32[32,1,128]{2,1,0:T(1,128)}), f32[32,1,128]{2,1,0:T(1,128)S(1)}, u32[]{:S(2)}, u32[]{:S(2)}) async-start(f32[32,1,128]{2,1,0:T(1,128)} %bitcast.10), calls=%async_computation.5 | async-start | bytes 32768 | tf_op jit(solution)/shard_map/all_to_all | solution.py:472
  126.2 0.8 shard_map.120
  127.0 6.1 %all-to-all-done.5 = f32[32,1,128]{2,1,0:T(1,128)S(1)} async-done(((f32[32,1,128]{2,1,0:T(1,128)}), f32[32,1,128]{2,1,0:T(1,128)S(1)}, u32[]{:S(2)}, u32[]{:S(2)}) %all-to-all-start.5) | async-done | bytes 16416 | tf_op jit(solution)/shard_map/all_to_all | solution.py:472
  133.2 0.6 shard_map.121
  (6 shorter events, 0.1 us)
Async XLA Ops:
  1.3 34.1 %copy-start = (bf16[64,64,128]{2,1,0:T(8,128)(2,1)S(1)}, bf16[64,64,128]{2,1,0:T(8,128)(2,1)}, u32[]{:S(2)}) copy-start(bf16[64,64,128]{2,1,0:T(8,128)(2,1)} %local_inverse.1) | copy-start | bytes 3145732
  1.3 34.1 %copy-start.3 = (f32[64,128]{1,0:T(8,128)S(1)}, f32[64,128]{1,0:T(8,128)}, u32[]{:S(2)}) copy-start(f32[64,128]{1,0:T(8,128)} %field.3) | copy-start | bytes 98308
  1.3 34.1 %copy-start.5 = (s32[1,2,32]{2,1,0:T(2,128)S(1)}, s32[1,2,32]{2,1,0:T(2,128)}, u32[]{:S(2)}) copy-start(s32[1,2,32]{2,1,0:T(2,128)} %margin_rows.5) | copy-start | bytes 772
  4.3 31.1 %collective-permute-start.1 = (f32[64,16,128]{2,1,0:T(8,128)}, f32[64,16,128]{2,1,0:T(8,128)S(1)}, u32[]{:S(2)}, u32[]{:S(2)}) collective-permute-start(f32[64,16,128]{2,1,0:T(8,128)} %get-tuple-element.55), channel_id=1, source_target_pairs={{0,8},{1,9},{2,10},{3,11},{8,16},{9,17},{10,18},{11,19},{12,4},{13... | collective-permute-start | bytes 1572872 | tf_op jit(solution)/shard_map/ppermute | solution.py:506
  33.9 2.4 %copy-start.1 = (bf16[64,64,128]{2,1,0:T(8,128)(2,1)S(1)}, bf16[64,64,128]{2,1,0:T(8,128)(2,1)}, u32[]{:S(2)}) copy-start(bf16[64,64,128]{2,1,0:T(8,128)(2,1)} %basis.9) | copy-start | bytes 3145732
  33.9 2.4 %copy-start.2 = (f32[64,2048]{1,0:T(8,128)S(1)}, f32[64,2048]{1,0:T(8,128)}, u32[]{:S(2)}) copy-start(f32[64,2048]{1,0:T(8,128)} %coarse.5) | copy-start | bytes 1572868
  33.9 2.4 %collective-permute-start = (f32[16,128]{1,0:T(8,128)S(1)}, f32[16,128]{1,0:T(8,128)S(1)}, u32[]{:S(2)}, u32[]{:S(2)}) collective-permute-start(f32[16,128]{1,0:T(8,128)S(1)} %bitcast_reduce_fusion.2.table), channel_id=1, source_target_pairs={{0,8},{8,0},{1,9},{9,1},{2,10},{10,2},{3,11},{11,3},{4,12},{12,4},... | collective-permute-start | bytes 24584 | tf_op jit(solution)/shard_map/ppermute | solution.py:476
  35.4 21.4 %slice-start = ((s8[7340032]{0:T(1024)(128)(4,1)}), s8[4194304]{0:T(1024)(128)(4,1)S(1)}, s32[]{:S(2)}) async-start(s8[7340032]{0:T(1024)(128)(4,1)} %bitcast.25), calls=%async_computation.6 | async-start | bytes 8388608
  36.3 20.5 %slice-start.1 = ((s8[7340032]{0:T(1024)(128)(4,1)}), s8[3145728]{0:T(1024)(128)(4,1)S(1)}, s32[]{:S(2)}) async-start(s8[7340032]{0:T(1024)(128)(4,1)} %bitcast.25), calls=%async_computation.7 | async-start | bytes 6291456
  36.3 20.5 %copy-start.4 = (s32[7,128]{1,0:T(8,128)S(1)}, s32[7,128]{1,0:T(8,128)}, u32[]{:S(2)}) copy-start(s32[7,128]{1,0:T(8,128)} %columns.3) | copy-start | bytes 10756
  36.9 5.1 %collective-permute-start.2 = (f32[16,128]{1,0:T(8,128)S(1)}, f32[16,128]{1,0:T(8,128)S(1)}, u32[]{:S(2)}, u32[]{:S(2)}) collective-permute-start(f32[16,128]{1,0:T(8,128)S(1)} %get-tuple-element.58), channel_id=1, source_target_pairs={{4,12},{5,13},{6,14},{7,15},{8,0},{9,1},{10,2},{11,3},{12,20},{13,... | collective-permute-start | bytes 24584 | tf_op jit(solution)/shard_map/ppermute | solution.py:479
  76.2 2.6 %collective-permute-start.3 = (f32[16,128]{1,0:T(8,128)S(1)}, f32[16,128]{1,0:T(8,128)S(1)}, u32[]{:S(2)}, u32[]{:S(2)}) collective-permute-start(f32[16,128]{1,0:T(8,128)S(1)} %bitcast_reduce_fusion.1.table), channel_id=1, source_target_pairs={{0,8},{8,0},{1,9},{9,1},{2,10},{10,2},{3,11},{11,3},{4,12},{12,4},... | collective-permute-start | bytes 24584 | tf_op jit(solution)/shard_map/ppermute | solution.py:476
  79.5 5.0 %collective-permute-start.4 = (f32[16,128]{1,0:T(8,128)S(1)}, f32[16,128]{1,0:T(8,128)S(1)}, u32[]{:S(2)}, u32[]{:S(2)}) collective-permute-start(f32[16,128]{1,0:T(8,128)S(1)} %get-tuple-element.65), channel_id=1, source_target_pairs={{4,12},{5,13},{6,14},{7,15},{8,0},{9,1},{10,2},{11,3},{12,20},{13,... | collective-permute-start | bytes 24584 | tf_op jit(solution)/shard_map/ppermute | solution.py:479
  118.9 2.6 %collective-permute-start.5 = (f32[16,128]{1,0:T(8,128)S(1)}, f32[16,128]{1,0:T(8,128)S(1)}, u32[]{:S(2)}, u32[]{:S(2)}) collective-permute-start(f32[16,128]{1,0:T(8,128)S(1)} %bitcast_reduce_fusion.table), channel_id=1, source_target_pairs={{0,8},{8,0},{1,9},{9,1},{2,10},{10,2},{3,11},{11,3},{4,12},{12,4},... | collective-permute-start | bytes 24584 | tf_op jit(solution)/shard_map/ppermute | solution.py:476
  122.3 10.8 %all-to-all-start.5 = ((f32[32,1,128]{2,1,0:T(1,128)}), f32[32,1,128]{2,1,0:T(1,128)S(1)}, u32[]{:S(2)}, u32[]{:S(2)}) async-start(f32[32,1,128]{2,1,0:T(1,128)} %bitcast.10), calls=%async_computation.5 | async-start | bytes 32768 | tf_op jit(solution)/shard_map/all_to_all | solution.py:472
